TPU v7x, 32 devices: a whole 2x2x4 slice. The times are simulated.
32 devices in a mesh: row: 4 (over y, x), col: 8 (over z, core).
Axes of the slice: x: 2, y: 2, z: 4, core: 2. Of those that a mesh axis runs over, the one named last changes fastest.
Arguments:
- tiles: bfloat16 [4, 8, 32, 256, 256], P('row', 'col'), may hold values from -6 to 6
- tile_ids: int32 [4, 8, 2, 32], P('row', 'col'), may hold values from 0 to 7, as said below
- tile_count: int32 [4, 8], P('row', 'col'), may hold values from 8 to 32
- query_degree: int32 [8192], P('row'), may hold values from 1 to 32
- product_degree: int32 [16384], P('col'), may hold values from 1 to 32
- panel: float32 [64, 16384], P(None, ('col', 'row')), may hold values from -6 to 6
Outputs:
- basis: float32 [64, 16384], P(None, ('col', 'row'))
Inputs may be any that keep to these rules, and one draw needn't show every extreme that they name: `tile_ids`: on each device the 32 (tile row, tile column) pairs are distinct; tile row is below 8 and tile column below 8.
All inputs are finite; a program needn't handle non-finite values.
Results may differ from a plain program's by a relative error of at most 0.0042.
Values may be sent and summed in bfloat16 or wider, within the bound.
No kernel may reach another device: no remote copies, remote signals or barrier semaphores. Data moves between devices by JAX's collectives and lax.ppermute only.
A program may use at most 64 MiB of HBM per device.

v0:
```python
import math

import jax
import jax.numpy as jnp
from jax import lax
from jax.sharding import PartitionSpec as P

ITERS = 2


HIGH = lax.Precision.HIGHEST


def orthonormal(lifted, gram):
    lower = jnp.linalg.cholesky(gram)
    return lax.linalg.triangular_solve(lower, lifted, left_side=True, lower=True)


def shards(tiles, tile_ids, tile_count, query_degree, product_degree, panel):
    tile_set = tiles[0, 0]
    slot_ids = tile_ids[0, 0]
    live_count = tile_count[0, 0]
    slots = tile_set.shape[0]
    side = tile_set.shape[1]
    width = panel.shape[0]
    query_tiles = query_degree.shape[0] // side
    product_tiles = product_degree.shape[0] // side
    live_slot = (jnp.arange(slots, dtype=jnp.int32) < live_count).astype(jnp.float32)
    row_hot = (slot_ids[0][:, None] == jnp.arange(query_tiles, dtype=jnp.int32)[None, :]).astype(
        jnp.float32
    ) * live_slot[:, None]
    col_hot = (slot_ids[1][:, None] == jnp.arange(product_tiles, dtype=jnp.int32)[None, :]).astype(
        jnp.float32
    ) * live_slot[:, None]
    qscale = 1.0 / jnp.sqrt(query_degree.astype(jnp.float32))
    pscale = 1.0 / jnp.sqrt(product_degree.astype(jnp.float32))
    row_at = lax.axis_index("row")
    col_at = lax.axis_index("col")
    share = panel.shape[1]
    my_pscale = lax.dynamic_slice_in_dim(pscale, row_at * share, share)
    root_count = math.sqrt(product_degree.shape[0] * lax.axis_size("col"))
    current = panel
    for iteration in range(ITERS):
        scaled = (current * my_pscale[None, :]).astype(jnp.bfloat16)
        scaled_block = lax.all_gather(scaled, "row", axis=1, tiled=True)
        picked = jnp.take(scaled_block.reshape(width, product_tiles, side), slot_ids[1], axis=1)
        products = jnp.einsum("rkj,kij->kri", picked, tile_set, preferred_element_type=jnp.float32)
        partial_sum = jnp.einsum("kq,kri->rqi", row_hot, products, precision=HIGH).reshape(
            width, query_tiles * side
        )
        query_share = lax.psum_scatter(partial_sum, "col", scatter_dimension=1, tiled=True)
        columns = query_share.shape[1]
        my_qscale = lax.dynamic_slice_in_dim(qscale, col_at * columns, columns)
        rounded = (query_share * my_qscale[None, :]).astype(jnp.bfloat16)
        query_block = lax.all_gather(rounded, "col", axis=1, tiled=True)
        backward_picked = jnp.take(
            query_block.reshape(width, query_tiles, side), slot_ids[0], axis=1
        )
        backward_products = jnp.einsum(
            "rki,kij->krj", backward_picked, tile_set, preferred_element_type=jnp.float32
        )
        lifted = (
            lax.psum_scatter(
                jnp.einsum("kp,krj->rpj", col_hot, backward_products, precision=HIGH).reshape(
                    width, product_tiles * side
                ),
                "row",
                scatter_dimension=1,
                tiled=True,
            )
            * my_pscale[None, :]
        )
        gram = lax.psum(jnp.einsum("ri,si->rs", lifted, lifted, precision=HIGH), ("row", "col"))
        current = orthonormal(lifted, gram)
    return current * root_count


def solution(mesh):
    in_specs = (
        P("row", "col", None, None, None),
        P("row", "col", None, None),
        P("row", "col"),
        P("row"),
        P("col"),
        P(None, ("col", "row")),
    )
    out_specs = P(None, ("col", "row"))
    return jax.shard_map(shards, mesh=mesh, in_specs=in_specs, out_specs=out_specs, check_vma=False)
```

profile of v0, /device:TPU:0, one launch (start us, length us, event | category | flops | bytes accessed | tf_op | source)
XLA Modules:
  0.0 313.9 jit_solution(18196625617586841470)
XLA Ops:
  9.5 0.9 multiply_convert_fusion
  10.4 10.4 %all_gather.12 = bf16[64,2048]{1,0:T(8,128)(2,1)S(1)} all-gather(bf16[64,512]{1,0:T(8,128)(2,1)S(1)} %multiply_convert_fusion), channel_id=1, replica_groups=mesh['row'=4,'col'=8] {'row'}, dimensions={1}, use_global_device_ids=true | all-gather | bytes 327680 | tf_op jit(solution)/shard_map/all_gather | solution.py:45
  21.5 3.6 %fusion.6 = f32[32,64,256]{2,1,0:T(8,128)S(1)} fusion(bf16[1,1,32,256,256]{4,3,2,1,0:T(8,128)(2,1)} %param.11, bf16[32,64,256]{2,1,0:T(8,128)(2,1)S(1)} %gather_fusion, pred[32]{0:T(512)(128)(4,1)S(1)} %get-tuple-element.14), kind=kOutput, calls=%fused_computation.10 | convolution fusion | flops 268959744 | bytes 7340064 | tf_op jit(solution)/shard_map/rkj,kij->kri/dot_general | solution.py:47
  25.1 2.4 fusion.14
  27.5 1.0 copy.35
  29.3 30.5 %reduce-scatter.5.cloned.1.call-done = f32[64,256]{1,0:T(8,128)} async-done(((f32[64,2048]{1,0:T(8,128)}), f32[64,256]{1,0:T(8,128)}) %reduce-scatter.5.cloned.1.call-update) | async-done | bytes 65552 | tf_op jit(solution)/shard_map/reduce_scatter | solution.py:51
  59.8 0.8 multiply_convert_fusion.2
  60.7 14.2 %all_gather.13 = bf16[64,2048]{1,0:T(8,128)(2,1)S(1)} all-gather(bf16[64,256]{1,0:T(8,128)(2,1)S(1)} %multiply_convert_fusion.2), channel_id=1, replica_groups=mesh['row'=4,'col'=8] {'col'}, dimensions={1}, use_global_device_ids=true | all-gather | bytes 294912 | tf_op jit(solution)/shard_map/all_gather | solution.py:55
  75.5 3.1 fusion.4
  78.6 2.4 fusion.12
  81.0 1.0 copy.36
  82.0 23.1 %reduce-scatter.7.cloned.1.call-done = f32[64,512]{1,0:T(8,128)} async-done(((f32[64,2048]{1,0:T(8,128)}), f32[64,512]{1,0:T(8,128)}) %reduce-scatter.7.cloned.1.call-update) | async-done | bytes 131088 | tf_op jit(solution)/shard_map/reduce_scatter | solution.py:63
  105.1 1.2 fusion.37
  106.3 39.5 %psum.14 = f32[64,64]{0,1:T(8,128)S(1)} all-reduce(f32[64,64]{0,1:T(8,128)S(1)} %fusion.37), channel_id=1, replica_groups=mesh['row'=4,'col'=8] {'row','col'}, use_global_device_ids=true, to_apply=%region_2.4 | all-reduce | flops 4096 | bytes 32768 | tf_op jit(solution)/shard_map/psum | solution.py:73
  145.9 5.8 %cholesky.44 = f32[64,64]{1,0:T(8,128)S(1)} custom-call(f32[64,64]{1,0:T(8,128)S(1)} %fusion.48), custom_call_target="Cholesky" | custom-call | tf_op jit(solution)/shard_map/jit(cholesky)/cholesky | solution.py:15
  153.1 4.9 %custom-call.6 = f32[1,64,64]{1,2,0:T(8,128)S(1)} custom-call(f32[1,64,64]{2,1,0:T(8,128)S(1)} %fusion.43), custom_call_target="InvertDiagBlocksLowerTriangular" | custom-call | tf_op jit(solution)/shard_map/triangular_solve/custom-call.0 | solution.py:16
  158.0 1.2 fusion.16
  159.3 10.3 %all_gather.14 = bf16[64,2048]{1,0:T(8,128)(2,1)S(1)} all-gather(bf16[64,512]{1,0:T(8,128)(2,1)S(1)} %fusion.16), channel_id=1, replica_groups=mesh['row'=4,'col'=8] {'row'}, dimensions={1}, use_global_device_ids=true | all-gather | bytes 327680 | tf_op jit(solution)/shard_map/all_gather | solution.py:45
  170.2 3.6 %fusion.2 = f32[32,64,256]{2,1,0:T(8,128)S(1)} fusion(bf16[1,1,32,256,256]{4,3,2,1,0:T(8,128)(2,1)} %param.11, bf16[32,64,256]{2,1,0:T(8,128)(2,1)S(1)} %gather_fusion.2, pred[32]{0:T(512)(128)(4,1)S(1)} %get-tuple-element.14), kind=kOutput, calls=%fused_computation.6 | convolution fusion | flops 268959744 | bytes 7340064 | tf_op jit(solution)/shard_map/rkj,kij->kri/dot_general | solution.py:47
  173.8 2.4 fusion.10
  176.2 1.0 copy.37
  177.2 30.1 %reduce-scatter.9.cloned.1.call-done = f32[64,256]{1,0:T(8,128)} async-done(((f32[64,2048]{1,0:T(8,128)}), f32[64,256]{1,0:T(8,128)}) %reduce-scatter.9.cloned.1.call-update) | async-done | bytes 65552 | tf_op jit(solution)/shard_map/reduce_scatter | solution.py:51
  208.2 14.2 %all_gather.15 = bf16[64,2048]{1,0:T(8,128)(2,1)S(1)} all-gather(bf16[64,256]{1,0:T(8,128)(2,1)S(1)} %multiply_convert_fusion.1), channel_id=1, replica_groups=mesh['row'=4,'col'=8] {'col'}, dimensions={1}, use_global_device_ids=true | all-gather | bytes 294912 | tf_op jit(solution)/shard_map/all_gather | solution.py:55
  223.0 3.1 fusion
  226.1 2.4 fusion.8
  228.4 1.0 copy.38
  229.4 23.1 %reduce-scatter.11.cloned.1.call-done = f32[64,512]{1,0:T(8,128)} async-done(((f32[64,2048]{1,0:T(8,128)}), f32[64,512]{1,0:T(8,128)}) %reduce-scatter.11.cloned.1.call-update) | async-done | bytes 131088 | tf_op jit(solution)/shard_map/reduce_scatter | solution.py:63
  252.5 1.2 fusion.34
  253.8 39.5 %psum.15 = f32[64,64]{0,1:T(8,128)S(1)} all-reduce(f32[64,64]{0,1:T(8,128)S(1)} %fusion.34), channel_id=1, replica_groups=mesh['row'=4,'col'=8] {'row','col'}, use_global_device_ids=true, to_apply=%region_7.11 | all-reduce | flops 4096 | bytes 32768 | tf_op jit(solution)/shard_map/psum | solution.py:73
  293.4 5.8 %cholesky.55 = f32[64,64]{1,0:T(8,128)S(1)} custom-call(f32[64,64]{1,0:T(8,128)S(1)} %fusion.46), custom_call_target="Cholesky" | custom-call | tf_op jit(solution)/shard_map/jit(cholesky)/cholesky | solution.py:15
  300.6 4.9 %custom-call.7 = f32[1,64,64]{1,2,0:T(8,128)S(1)} custom-call(f32[1,64,64]{2,1,0:T(8,128)S(1)} %fusion.44), custom_call_target="InvertDiagBlocksLowerTriangular" | custom-call | tf_op jit(solution)/shard_map/triangular_solve/custom-call.0 | solution.py:16
  305.5 1.9 convolution_multiply_fusion
  (34 shorter events, 9.5 us)
Async XLA Ops:
  6.5 53.3 %reduce-scatter.5.cloned.1.call-start = ((), (), s32[]{:S(2)}) async-start(), calls=%async_computation.4 | async-start | bytes 589824 | tf_op jit(solution)/shard_map/reduce_scatter | solution.py:51
  28.5 76.6 %reduce-scatter.7.cloned.1.call-start = ((), (), s32[]{:S(2)}) async-start(), calls=%async_computation.5 | async-start | bytes 655360 | tf_op jit(solution)/shard_map/reduce_scatter | solution.py:63
  81.9 125.4 %reduce-scatter.9.cloned.1.call-start = ((), (), s32[]{:S(2)}) async-start(), calls=%async_computation.6 | async-start | bytes 589824 | tf_op jit(solution)/shard_map/reduce_scatter | solution.py:51
  177.1 75.4 %reduce-scatter.11.cloned.1.call-start = ((), (), s32[]{:S(2)}) async-start(), calls=%async_computation.7 | async-start | bytes 655360 | tf_op jit(solution)/shard_map/reduce_scatter | solution.py:63
Sparse Core Ops, SparseCore 0:
  28.6 31.2 reduce-scatter.4
  82.1 22.9 reduce-scatter.6
  177.3 29.9 reduce-scatter.8
  229.5 22.9 reduce-scatter.10
where the time goes:
time: 315 us; the launch traced here: 314 us
  blocking collectives  128 us (41%)
  waiting for transfers between devices  107 us (34%)
  other arithmetic  29.1 us (9%)
  matrix products  28.4 us (9%)
  between operations  14 us (4%)
  local copies, waits for them, and re-layouts  7.24 us (2%)
    psum x2, blocking collectives, shards(): lax.psum(jnp.einsum('ri,si->rs', lifted, lifted, precision=HIGH), ('row',...  79 us
    reduce_scatter x2, waiting for transfers between devices, shards(): lax.psum_scatter(partial_sum, 'col', scatter_dimension=1, tiled=True)  60.7 us
    reduce_scatter x2, waiting for transfers between devices, shards(): lax.psum_scatter(jnp.einsum('kp,krj->rpj', col_hot, backward_products, pr...  46.2 us
    all_gather x2, blocking collectives, shards(): query_block = lax.all_gather(rounded, 'col', axis=1, tiled=True)  28.4 us
    all_gather x2, blocking collectives, shards(): scaled_block = lax.all_gather(scaled, 'row', axis=1, tiled=True)  20.7 us
    another operation x6, other arithmetic, orthonormal(): lower = jnp.linalg.cholesky(gram)  13 us
    another operation x4, other arithmetic, orthonormal(): lax.linalg.triangular_solve(lower, lifted, left_side=True, lower=True)  11.1 us
    dot_general x2, matrix products, shards(): jnp.einsum('rkj,kij->kri', picked, tile_set, preferred_element_type=jnp.f...  7.18 us
  transfers between devices with their start and end apart: 4, of which 4 were waited for; matrix products, arithmetic and copies ran while one was open for 0% of the time, Pallas kernels for 0%

commit v1 on v0

v1 whole, which is shorter than its diff:
```python
import functools
import math

import jax
import jax.numpy as jnp
from jax import lax
from jax.experimental import pallas as pl
from jax.experimental.pallas import tpu as pltpu
from jax.sharding import PartitionSpec as P

ITERS = 2
GROUP = 8
PANEL_STEP = 4
HIGH = lax.Precision.HIGHEST
VMEM_BYTES = 40 * 1024 * 1024
NT = (((1,), (1,)), ((), ()))
NN = (((1,), (0,)), ((), ()))


def pack(block_refs, held, side):
    count, _, share = block_refs.shape
    for block in range(count):
        if share >= side:
            per = share // side
            for piece in range(per):
                held[block * per + piece] = block_refs[block, :, piece * side : (piece + 1) * side]
        else:
            per = side // share
            at = (block % per) * share
            held[block // per, :, at : at + share] = block_refs[block]


def unpack(total, out_ref, side):
    count, _, share = out_ref.shape
    for block in range(count):
        if share >= side:
            per = share // side
            for piece in range(per):
                out_ref[block, :, piece * side : (piece + 1) * side] = total[
                    block * per + piece
                ].astype(out_ref.dtype)
        else:
            per = side // share
            at = (block % per) * share
            out_ref[block] = total[block // per, :, at : at + share].astype(out_ref.dtype)


def product_body(source, target, dims, ids, live, block_ref, tile_ref, out_ref, held, total):
    side = tile_ref.shape[1]
    slots = tile_ref.shape[0]
    tiles = total.shape[0] - 1
    pack(block_ref, held, side)
    total[...] = jnp.zeros_like(total)
    count = live[0]

    def group(g, carry):
        for lane in range(GROUP):
            slot = g * GROUP + lane
            take = ids[source, slot]
            give = jnp.where(slot < count, ids[target, slot], tiles)
            total[give] += lax.dot_general(
                held[take], tile_ref[slot], dims, preferred_element_type=jnp.float32
            )
        return carry

    lax.fori_loop(0, jnp.minimum((count + GROUP - 1) // GROUP, slots // GROUP), group, 0)
    unpack(total, out_ref, side)


def product(blocks, tile_set, ids, live, source, target, dims, pieces, share, in_tiles, out_tiles, dtype):
    width = blocks.shape[1]
    slots, side, _ = tile_set.shape
    return pl.pallas_call(
        functools.partial(product_body, source, target, dims),
        out_shape=jax.ShapeDtypeStruct((pieces, width, share), dtype),
        grid_spec=pltpu.PrefetchScalarGridSpec(
            num_scalar_prefetch=2,
            grid=(),
            in_specs=[pl.BlockSpec(memory_space=pltpu.VMEM)] * 2,
            out_specs=pl.BlockSpec(memory_space=pltpu.VMEM),
            scratch_shapes=[
                pltpu.VMEM((in_tiles, width, side), jnp.bfloat16),
                pltpu.VMEM((out_tiles + 1, width, side), jnp.float32),
            ],
        ),
        compiler_params=pltpu.CompilerParams(vmem_limit_bytes=VMEM_BYTES),
        cost_estimate=pl.CostEstimate(
            flops=2 * slots * width * side * side, bytes_accessed=2 * slots * side * side, transcendentals=0
        ),
        name="product",
    )(ids, live, blocks, tile_set)


def lift_body(part_ref, scale_ref, lifted_ref, gram_ref):
    total = part_ref[0]
    for part in range(1, part_ref.shape[0]):
        total = total + part_ref[part]
    lifted = total * scale_ref[...]
    lifted_ref[...] = lifted
    gram_ref[...] = lax.dot_general(
        lifted, lifted, NT, precision=HIGH, preferred_element_type=jnp.float32
    )


def lift(parts, scale):
    _, width, share = parts.shape
    return pl.pallas_call(
        lift_body,
        out_shape=(
            jax.ShapeDtypeStruct((width, share), jnp.float32),
            jax.ShapeDtypeStruct((width, width), jnp.float32),
        ),
        compiler_params=pltpu.CompilerParams(vmem_limit_bytes=VMEM_BYTES),
        name="lift",
    )(parts, scale)


def inverse_factor(gram):
    width = gram.shape[0]
    rows = lax.broadcasted_iota(jnp.int32, (width, width), 0)
    cols = lax.broadcasted_iota(jnp.int32, (width, width), 1)
    work = jnp.concatenate([gram, (rows == cols).astype(jnp.float32)], axis=1)
    done = []
    for first in range(0, width, PANEL_STEP):
        base = first // 8 * 8
        height = width - base
        ids = lax.broadcasted_iota(jnp.int32, (height, 2 * width), 0) + base
        columns = [
            jnp.broadcast_to(work[:, first + j : first + j + 1], (height, 2 * width))
            for j in range(PANEL_STEP)
        ]
        for j in range(PANEL_STEP):
            k = first + j
            at = k - base
            pivot = columns[j][at : at + 1, :]
            factor = jnp.where(ids > k, columns[j] * (1.0 / pivot), 0.0)
            row = work[at : at + 1, :]
            done.append(row * lax.rsqrt(pivot))
            work = work - factor * row
            for later in range(j + 1, PANEL_STEP):
                columns[later] = columns[later] - factor * columns[later][at : at + 1, :]
        after = (first + PANEL_STEP) // 8 * 8
        if after > base:
            work = work[after - base :, :]
    return jnp.concatenate(done, axis=0)[:, width:]


def solve_body(after, gram_ref, lifted_ref, scale_ref, out_ref):
    gram = gram_ref[0]
    for part in range(1, gram_ref.shape[0]):
        gram = gram + gram_ref[part]
    current = lax.dot_general(
        inverse_factor(gram), lifted_ref[...], NN, precision=HIGH, preferred_element_type=jnp.float32
    )
    if after is None:
        out_ref[...] = (current * scale_ref[...]).astype(out_ref.dtype)
    else:
        out_ref[...] = current * after


def solve(grams, lifted, scale, after):
    return pl.pallas_call(
        functools.partial(solve_body, after),
        out_shape=jax.ShapeDtypeStruct(lifted.shape, jnp.bfloat16 if after is None else jnp.float32),
        compiler_params=pltpu.CompilerParams(vmem_limit_bytes=VMEM_BYTES),
        name="solve",
    )(grams, lifted, scale)


def exchange(parts, axis):
    return lax.all_to_all(parts, axis, 0, 0)


def gather_by_exchange(block, axis):
    count = lax.axis_size(axis)
    return exchange(jnp.broadcast_to(block[None], (count, *block.shape)), axis)


def gather_by_permute(block, axis):
    count = lax.axis_size(axis)
    at = lax.axis_index(axis)
    pieces = [block]
    for step in range(1, count):
        pieces.append(
            lax.ppermute(block, axis, [(i, (i + step) % count) for i in range(count)])
        )
    order = lax.rem(at - jnp.arange(count, dtype=jnp.int32) + count, count)
    return jnp.stack(pieces)[order]


def shards(tiles, tile_ids, tile_count, query_degree, product_degree, panel):
    tile_set = tiles[0, 0]
    ids = tile_ids[0, 0]
    live = tile_count[0]
    side = tile_set.shape[1]
    queries, products = query_degree.shape[0], product_degree.shape[0]
    query_tiles, product_tiles = queries // side, products // side
    n_row, n_col = lax.axis_size("row"), lax.axis_size("col")
    row_at, col_at = lax.axis_index("row"), lax.axis_index("col")
    share = panel.shape[1]
    columns = queries // n_col
    my_pscale = 1.0 / jnp.sqrt(
        lax.dynamic_slice_in_dim(product_degree, row_at * share, share).astype(jnp.float32)
    )[None, :]
    my_qscale = 1.0 / jnp.sqrt(
        lax.dynamic_slice_in_dim(query_degree, col_at * columns, columns).astype(jnp.float32)
    )[None, :]
    root_count = math.sqrt(products * n_col)
    scaled = (panel * my_pscale).astype(jnp.bfloat16)
    for iteration in range(ITERS):
        last = iteration == ITERS - 1
        if iteration == 0:
            blocks = gather_by_permute(scaled, "row")
        else:
            blocks = lax.all_gather(scaled, "row")
        sums = product(
            blocks, tile_set, ids, live, 1, 0, NT, n_col, columns, product_tiles, query_tiles, jnp.bfloat16
        )
        query_sum = jnp.sum(exchange(sums, "col").astype(jnp.float32), axis=0)
        rounded = (query_sum * my_qscale).astype(jnp.bfloat16)
        if iteration == 0:
            blocks = lax.all_gather(rounded, "col")
        else:
            blocks = gather_by_exchange(rounded, "col")
        sums = product(
            blocks, tile_set, ids, live, 0, 1, NN, n_row, share, query_tiles, product_tiles, jnp.float32
        )
        lifted, gram = lift(exchange(sums, "row"), my_pscale)
        if iteration == 0:
            grams = lax.all_gather(gram, ("row", "col"))
        else:
            grams = gather_by_exchange(jnp.sum(gather_by_exchange(gram, "row"), axis=0), "col")
        scaled = solve(grams, lifted, my_pscale, root_count if last else None)
    return scaled


def solution(mesh):
    in_specs = (
        P("row", "col", None, None, None),
        P("row", "col", None, None),
        P("row", "col"),
        P("row"),
        P("col"),
        P(None, ("col", "row")),
    )
    out_specs = P(None, ("col", "row"))
    return jax.shard_map(shards, mesh=mesh, in_specs=in_specs, out_specs=out_specs, check_vma=False)
```

time: 315 us -> 180 us (0.57)
  waiting for transfers between devices: 107 us -> 10.2 us
  matrix products: 28.4 us -> 0 us
  other arithmetic: 29.1 us -> 5.29 us
  Pallas kernels: 0 us -> 16.6 us
  between operations: 14 us -> 0.83 us
  starting transfers between devices: 0.13 us -> 9.92 us
    reduce_scatter x4 -> x0, waiting for transfers between devices: 107 us -> none  [the longest x2 60.7 us: shards(): lax.psum_scatter(partial_sum, 'col', scatter_dimension=1, tiled=True)]
    psum x2 -> x0, blocking collectives: 79 us -> none  [shards(): lax.psum(jnp.einsum('ri,si->rs', lifted, lifted, precision=HIGH), ('row',...]
    all_to_all x0 -> x6, blocking collectives: none -> 64.3 us  [exchange(): return lax.all_to_all(parts, axis, 0, 0)]
    dot_general x10 -> x0, matrix products: 25.3 us -> none  [the longest x2 7.18 us: shards(): jnp.einsum('rkj,kij->kri', picked, tile_set, preferred_element_type=jnp.f...]
    another operation x10 -> x2, other arithmetic: 24.1 us -> 0.95 us  [gather_by_permute(): return jnp.stack(pieces)[order]]
    pallas_call x0 -> x8, Pallas kernels: none -> 16.6 us  [the longest x4 9.35 us: product(): pl.pallas_call(functools.partial(product_body, source, target, dims), out...]
    all_gather x4 -> x3, blocking collectives: 49.1 us -> 65.6 us  [the longest x1 42.4 us: shards(): grams = lax.all_gather(gram, ('row', 'col'))]
    all_to_all x0 -> x1, waiting for transfers between devices: none -> 8.98 us  [exchange(): return lax.all_to_all(parts, axis, 0, 0)]
  transfers between devices with their start and end apart: 4 -> 4, of which waited for: 4 -> 2; matrix products, arithmetic and copies ran while one was open for 0% -> 1% of each run, Pallas kernels for 0% -> 0%
where the time goes in v1:
time: 180 us; the launch traced here: 179 us
  blocking collectives  130 us (72%)
  Pallas kernels  16.6 us (9%)
  waiting for transfers between devices  10.2 us (6%)
  starting transfers between devices  9.92 us (6%)
  local copies, waits for them, and re-layouts  6.71 us (4%)
  other arithmetic  5.29 us (3%)
    all_to_all x6, blocking collectives, exchange(): return lax.all_to_all(parts, axis, 0, 0)  64.3 us
    all_gather x1, blocking collectives, shards(): grams = lax.all_gather(gram, ('row', 'col'))  42.4 us
    all_gather x1, blocking collectives, shards(): blocks = lax.all_gather(rounded, 'col')  14.2 us
    pallas_call x4, Pallas kernels, product(): pl.pallas_call(functools.partial(product_body, source, target, dims), out...  9.35 us
    all_to_all x1, waiting for transfers between devices, exchange(): return lax.all_to_all(parts, axis, 0, 0)  8.98 us
    all_gather x1, blocking collectives, shards(): blocks = lax.all_gather(scaled, 'row')  8.92 us
    pallas_call x2, Pallas kernels, solve(): pl.pallas_call(functools.partial(solve_body, after), out_shape=jax.ShapeD...  6.74 us
    ppermute x3, starting transfers between devices, gather_by_permute(): lax.ppermute(block, axis, [(i, (i + step) % count) for i in range(count)])  5.94 us
  transfers between devices with their start and end apart: 4, of which 2 were waited for; matrix products, arithmetic and copies ran while one was open for 1% of the time, Pallas kernels for 0%

profile of v1, /device:TPU:0, one launch (start us, length us, event | category | flops | bytes accessed | tf_op | source)
XLA Modules:
  0.0 179.5 jit_solution(2703398844249934213)
XLA Ops:
  0.0 0.8 convert_rsqrt_fusion
  0.8 0.9 multiply_convert_fusion
  1.7 3.0 %collective-permute-start = (bf16[64,512]{1,0:T(8,128)(2,1)S(1)}, bf16[64,512]{1,0:T(8,128)(2,1)S(1)}, u32[]{:S(2)}, u32[]{:S(2)}) collective-permute-start(bf16[64,512]{1,0:T(8,128)(2,1)S(1)} %multiply_convert_fusion), channel_id=1, source_target_pairs={{0,8},{8,16},{16,24},{24,0},{1,9},{9,17},{17,25},{25,1},{2,10},{10... | collective-permute-start | bytes 196616 | tf_op jit(solution)/shard_map/ppermute | solution.py:185
  4.7 1.5 collective-permute-start.1
  6.2 1.4 collective-permute-start.2
  7.6 0.9 fusion.3
  9.2 1.2 collective-permute-done.2
  10.5 0.6 gather_fusion
  11.1 2.2 %copy-done = bf16[1,1,32,256,256]{4,3,2,1,0:T(8,128)(2,1)S(1)} copy-done((bf16[1,1,32,256,256]{4,3,2,1,0:T(8,128)(2,1)S(1)}, bf16[1,1,32,256,256]{4,3,2,1,0:T(8,128)(2,1)}, u32[]{:S(2)}) %copy-start) | copy-done | bytes 4194328
  13.3 0.7 copy-done.3
  13.9 3.1 %product.4 = bf16[8,64,256]{2,1,0:T(8,128)(2,1)} custom-call(s32[2,32]{1,0:T(2,128)S(1)} %bitcast.31, s32[1]{0:T(128)} %bitcast.17.live, bf16[4,64,512]{2,1,0:T(8,128)(2,1)S(1)} %gather_fusion, bf16[32,256,256]{2,1,0:T(8,128)(2,1)S(1)} %bitcast.21), custom_call_target="tpu_custom_call" | custom-call | flops 268435456 | bytes 4194304 | tf_op jit(solution)/shard_map/product/pallas_call | solution.py:73
  17.1 4.0 %all-to-all-start = ((bf16[8,64,256]{2,1,0:T(8,128)(2,1)}), bf16[8,64,256]{2,1,0:T(8,128)(2,1)S(1)}, u32[]{:S(2)}, u32[]{:S(2)}) async-start(bf16[8,64,256]{2,1,0:T(8,128)(2,1)} %product.4), calls=%async_computation | async-start | bytes 524288 | tf_op jit(solution)/shard_map/all_to_all | solution.py:171
  21.1 0.8 convert_rsqrt_fusion.1
  21.8 9.0 %all-to-all-done = bf16[8,64,256]{2,1,0:T(8,128)(2,1)S(1)} async-done(((bf16[8,64,256]{2,1,0:T(8,128)(2,1)}), bf16[8,64,256]{2,1,0:T(8,128)(2,1)S(1)}, u32[]{:S(2)}, u32[]{:S(2)}) %all-to-all-start) | async-done | bytes 262176 | tf_op jit(solution)/shard_map/all_to_all | solution.py:171
  30.9 14.2 %all_gather.16.block_ref = bf16[8,64,256]{2,1,0:T(8,128)(2,1)S(1)} all-gather(bf16[1,64,256]{2,1,0:T(8,128)(2,1)S(1)} %fusion), channel_id=1, replica_groups=mesh['row'=4,'col'=8] {'col'}, dimensions={0}, use_global_device_ids=true | all-gather | bytes 294912 | tf_op jit(solution)/shard_map/all_gather | solution.py:222
  45.1 2.2 %copy-done.1 = bf16[1,1,32,256,256]{4,3,2,1,0:T(8,128)(2,1)S(1)} copy-done((bf16[1,1,32,256,256]{4,3,2,1,0:T(8,128)(2,1)S(1)}, bf16[1,1,32,256,256]{4,3,2,1,0:T(8,128)(2,1)}, u32[]{:S(2)}) %copy-start.1) | copy-done | bytes 4194328
  47.3 1.9 %product.5 = f32[4,64,512]{2,1,0:T(8,128)S(1)} custom-call(s32[2,32]{1,0:T(2,128)S(1)} %bitcast.32, s32[1]{0:T(128)} %bitcast.18.live, bf16[8,64,256]{2,1,0:T(8,128)(2,1)S(1)} %all_gather.16.block_ref, bf16[32,256,256]{2,1,0:T(8,128)(2,1)S(1)} %bitcast.22), custom_call_target="tpu_custom_call" | custom-call | flops 268435456 | bytes 4194304 | tf_op jit(solution)/shard_map/product/pallas_call | solution.py:73
  49.2 12.3 %all_to_all.35.part_ref = f32[4,64,512]{2,1,0:T(8,128)S(1)} all-to-all(f32[4,64,512]{2,1,0:T(8,128)S(1)} %product.5), channel_id=1, replica_groups=mesh['row'=4,'col'=8] {'row'}, dimensions={0} | all-to-all | bytes 1048576 | tf_op jit(solution)/shard_map/all_to_all | solution.py:171
  61.8 42.4 %all-gather = f32[2048,64]{1,0:T(8,128)S(1)} all-gather(f32[64,64]{1,0:T(8,128)S(1)} %get-tuple-element.9), channel_id=2, replica_groups=mesh['row'=4,'col'=8] {'row','col'}, dimensions={0}, use_global_device_ids=true | all-gather | bytes 540672 | tf_op jit(solution)/shard_map/all_gather | solution.py:230
  104.2 3.0 %solve.2 = bf16[64,512]{1,0:T(8,128)(2,1)S(1)} custom-call(f32[32,64,64]{2,1,0:T(8,128)S(1)} %bitcast.25, f32[64,512]{1,0:T(8,128)S(1)} %get-tuple-element.10.lifted_ref, f32[1,512]{1,0:T(1,128)S(1)} %bitcast.28), custom_call_target="tpu_custom_call" | custom-call | tf_op jit(solution)/shard_map/solve/pallas_call | solution.py:162
  107.2 8.9 %all-gather.1 = bf16[256,512]{1,0:T(8,128)(2,1)S(1)} all-gather(bf16[64,512]{1,0:T(8,128)(2,1)S(1)} %solve.2), channel_id=3, replica_groups=mesh['row'=4,'col'=8] {'row'}, dimensions={0}, use_global_device_ids=true | all-gather | bytes 327680 | tf_op jit(solution)/shard_map/all_gather | solution.py:215
  116.2 2.4 %product.6 = bf16[8,64,256]{2,1,0:T(8,128)(2,1)S(1)} custom-call(s32[2,32]{1,0:T(2,128)S(1)} %bitcast.33, s32[1]{0:T(128)} %bitcast.19.live, bf16[4,64,512]{2,1,0:T(8,128)(2,1)S(1)} %bitcast.26, bf16[32,256,256]{2,1,0:T(8,128)(2,1)S(1)} %bitcast.23), custom_call_target="tpu_custom_call" | custom-call | flops 268435456 | bytes 4194304 | tf_op jit(solution)/shard_map/product/pallas_call | solution.py:73
  118.6 12.1 %all_to_all.36 = bf16[8,64,256]{2,1,0:T(8,128)(2,1)S(1)} all-to-all(bf16[8,64,256]{2,1,0:T(8,128)(2,1)S(1)} %product.6), channel_id=1, replica_groups=mesh['row'=4,'col'=8] {'col'}, dimensions={0} | all-to-all | bytes 524288 | tf_op jit(solution)/shard_map/all_to_all | solution.py:171
  130.8 12.1 %all_to_all.37.block_ref = bf16[8,64,256]{2,1,0:T(8,128)(2,1)S(1)} all-to-all(bf16[8,64,256]{2,1,0:T(8,128)(2,1)S(1)} %broadcast_in_dim.6), channel_id=1, replica_groups=mesh['row'=4,'col'=8] {'col'}, dimensions={0} | all-to-all | bytes 524288 | tf_op jit(solution)/shard_map/all_to_all | solution.py:171
  143.0 1.9 %product.7 = f32[4,64,512]{2,1,0:T(8,128)S(1)} custom-call(s32[2,32]{1,0:T(2,128)S(1)} %bitcast.34, s32[1]{0:T(128)} %bitcast.20.live, bf16[8,64,256]{2,1,0:T(8,128)(2,1)S(1)} %all_to_all.37.block_ref, bf16[32,256,256]{2,1,0:T(8,128)(2,1)S(1)} %bitcast.24), custom_call_target="tpu_custom_call" | custom-call | flops 268435456 | bytes 4194304 | tf_op jit(solution)/shard_map/product/pallas_call | solution.py:73
  144.9 10.7 %all_to_all.38.part_ref = f32[4,64,512]{2,1,0:T(8,128)S(1)} all-to-all(f32[4,64,512]{2,1,0:T(8,128)S(1)} %product.7), channel_id=1, replica_groups=mesh['row'=4,'col'=8] {'row'}, dimensions={0} | all-to-all | bytes 1048576 | tf_op jit(solution)/shard_map/all_to_all | solution.py:171
  156.0 7.2 %all_to_all.39 = f32[4,1,4096]{2,1,0:T(1,128)S(1)} all-to-all(f32[4,1,4096]{2,1,0:T(1,128)S(1)} %reshape.101), channel_id=1, replica_groups=mesh['row'=4,'col'=8] {'row'}, dimensions={0} | all-to-all | bytes 131072 | tf_op jit(solution)/shard_map/all_to_all | solution.py:171
  163.2 0.5 broadcast.98
  163.7 0.8 reduce
  164.9 9.8 %all_to_all.40 = f32[8,1,4096]{2,1,0:T(1,128)S(1)} all-to-all(f32[8,1,4096]{2,1,0:T(1,128)S(1)} %reshape.103), channel_id=1, replica_groups=mesh['row'=4,'col'=8] {'col'}, dimensions={0} | all-to-all | bytes 262144 | tf_op jit(solution)/shard_map/all_to_all | solution.py:171
  174.7 1.0 reduce.1
  175.8 3.7 %solve.3 = f32[64,512]{1,0:T(8,128)} custom-call(f32[8,64,64]{2,1,0:T(8,128)S(1)} %reshape.104.gram_ref, f32[64,512]{1,0:T(8,128)S(1)} %get-tuple-element.12.lifted_ref, f32[1,512]{1,0:T(1,128)S(1)} %bitcast.30), custom_call_target="tpu_custom_call" | custom-call | tf_op jit(solution)/shard_map/solve/pallas_call | solution.py:162
  (24 shorter events, 1.3 us)
Async XLA Ops:
  1.7 7.5 %collective-permute-start = (bf16[64,512]{1,0:T(8,128)(2,1)S(1)}, bf16[64,512]{1,0:T(8,128)(2,1)S(1)}, u32[]{:S(2)}, u32[]{:S(2)}) collective-permute-start(bf16[64,512]{1,0:T(8,128)(2,1)S(1)} %multiply_convert_fusion), channel_id=1, source_target_pairs={{0,8},{8,16},{16,24},{24,0},{1,9},{9,17},{17,25},{25,1},{2,10},{10... | collective-permute-start | bytes 196616 | tf_op jit(solution)/shard_map/ppermute | solution.py:185
  4.7 4.6 %collective-permute-start.1 = (bf16[64,512]{1,0:T(8,128)(2,1)S(1)}, bf16[64,512]{1,0:T(8,128)(2,1)S(1)}, u32[]{:S(2)}, u32[]{:S(2)}) collective-permute-start(bf16[64,512]{1,0:T(8,128)(2,1)S(1)} %multiply_convert_fusion), channel_id=1, source_target_pairs={{0,16},{8,24},{16,0},{24,8},{1,17},{9,25},{17,1},{25,9},{2,18},{10... | collective-permute-start | bytes 196616 | tf_op jit(solution)/shard_map/ppermute | solution.py:185
  6.2 4.3 %collective-permute-start.2 = (bf16[64,512]{1,0:T(8,128)(2,1)S(1)}, bf16[64,512]{1,0:T(8,128)(2,1)S(1)}, u32[]{:S(2)}, u32[]{:S(2)}) collective-permute-start(bf16[64,512]{1,0:T(8,128)(2,1)S(1)} %multiply_convert_fusion), channel_id=1, source_target_pairs={{0,24},{8,0},{16,8},{24,16},{1,25},{9,1},{17,9},{25,17},{2,26},{10... | collective-permute-start | bytes 196616 | tf_op jit(solution)/shard_map/ppermute | solution.py:185
  11.1 2.2 %copy-start = (bf16[1,1,32,256,256]{4,3,2,1,0:T(8,128)(2,1)S(1)}, bf16[1,1,32,256,256]{4,3,2,1,0:T(8,128)(2,1)}, u32[]{:S(2)}) copy-start(bf16[1,1,32,256,256]{4,3,2,1,0:T(8,128)(2,1)} %param.6) | copy-start | bytes 12582916
  13.3 0.7 copy-start.3
  17.1 13.7 %all-to-all-start = ((bf16[8,64,256]{2,1,0:T(8,128)(2,1)}), bf16[8,64,256]{2,1,0:T(8,128)(2,1)S(1)}, u32[]{:S(2)}, u32[]{:S(2)}) async-start(bf16[8,64,256]{2,1,0:T(8,128)(2,1)} %product.4), calls=%async_computation | async-start | bytes 524288 | tf_op jit(solution)/shard_map/all_to_all | solution.py:171
  45.1 2.2 %copy-start.1 = (bf16[1,1,32,256,256]{4,3,2,1,0:T(8,128)(2,1)S(1)}, bf16[1,1,32,256,256]{4,3,2,1,0:T(8,128)(2,1)}, u32[]{:S(2)}) copy-start(bf16[1,1,32,256,256]{4,3,2,1,0:T(8,128)(2,1)} %param.6) | copy-start | bytes 12582916
  47.3 68.9 %copy-start.2 = (bf16[1,1,32,256,256]{4,3,2,1,0:T(8,128)(2,1)S(1)}, bf16[1,1,32,256,256]{4,3,2,1,0:T(8,128)(2,1)}, u32[]{:S(2)}) copy-start(bf16[1,1,32,256,256]{4,3,2,1,0:T(8,128)(2,1)} %param.6) | copy-start | bytes 12582916

commit v2 on v0

v2 whole, which is shorter than its diff:
```python
import functools
import math

import jax
import jax.numpy as jnp
from jax import lax
from jax.experimental import pallas as pl
from jax.experimental.pallas import tpu as pltpu
from jax.sharding import PartitionSpec as P

ITERS = 2
GROUP = 8
PANEL_STEP = 4
HIGH = lax.Precision.HIGHEST
VMEM_BYTES = 40 * 1024 * 1024
NT = (((1,), (1,)), ((), ()))
NN = (((1,), (0,)), ((), ()))

def inverse_factor(gram):
    width = gram.shape[0]
    rows = lax.broadcasted_iota(jnp.int32, (width, width), 0)
    cols = lax.broadcasted_iota(jnp.int32, (width, width), 1)
    work = jnp.concatenate([gram, (rows == cols).astype(jnp.float32)], axis=1)
    done = []
    for first in range(0, width, PANEL_STEP):
        base = first // 8 * 8
        height = width - base
        ids = lax.broadcasted_iota(jnp.int32, (height, 2 * width), 0) + base
        columns = [
            jnp.broadcast_to(work[:, first + j : first + j + 1], (height, 2 * width))
            for j in range(PANEL_STEP)
        ]
        for j in range(PANEL_STEP):
            k = first + j
            at = k - base
            pivot = columns[j][at : at + 1, :]
            factor = jnp.where(ids > k, columns[j] * (1.0 / pivot), 0.0)
            row = work[at : at + 1, :]
            done.append(row * lax.rsqrt(pivot))
            work = work - factor * row
            for later in range(j + 1, PANEL_STEP):
                columns[later] = columns[later] - factor * columns[later][at : at + 1, :]
        after = (first + PANEL_STEP) // 8 * 8
        if after > base:
            work = work[after - base :, :]
    return jnp.concatenate(done, axis=0)[:, width:]

WHOLE = pl.BlockSpec(memory_space=pltpu.VMEM)
SCALARS = pl.BlockSpec(memory_space=pltpu.SMEM)
AWAY = pl.BlockSpec(memory_space=pl.ANY)


def call(body, name, in_specs, out_shape, scratch=(), flops=0, moved=0):
    many = isinstance(out_shape, (tuple, list))
    return pl.pallas_call(
        body,
        out_shape=out_shape,
        in_specs=in_specs,
        out_specs=[WHOLE] * len(out_shape) if many else WHOLE,
        scratch_shapes=scratch,
        compiler_params=pltpu.CompilerParams(vmem_limit_bytes=VMEM_BYTES),
        cost_estimate=pl.CostEstimate(flops=flops, bytes_accessed=moved, transcendentals=0),
        name=name,
    )


def f32(*shape):
    return jax.ShapeDtypeStruct(shape, jnp.float32)


def bf16(*shape):
    return jax.ShapeDtypeStruct(shape, jnp.bfloat16)


def put(held, owner, value, side):
    share = value.shape[1]
    if share >= side:
        per = share // side
        for piece in range(per):
            held[owner * per + piece] = value[:, piece * side : (piece + 1) * side]
    else:
        per = side // share
        for at in range(per):

            @pl.when(owner % per == at)
            def _():
                held[owner // per, :, at * share : (at + 1) * share] = value


def get(total, owner, out_ref, side):
    share = out_ref.shape[1]
    if share >= side:
        per = share // side
        for piece in range(per):
            out_ref[:, piece * side : (piece + 1) * side] = total[owner * per + piece].astype(out_ref.dtype)
    else:
        per = side // share
        for at in range(per):

            @pl.when(owner % per == at)
            def _():
                out_ref[...] = total[owner // per, :, at * share : (at + 1) * share].astype(out_ref.dtype)


def emit(total, out_refs, me, side):
    count = len(out_refs)
    for step, out_ref in enumerate(out_refs):
        get(total, lax.rem(me + step, count), out_ref, side)


def collect(held, piece_refs, me, side):
    count = len(piece_refs)
    for step, piece_ref in enumerate(piece_refs):
        put(held, lax.rem(me + count - step, count), piece_ref[...], side)


def group_of(g, source, target, dims, count, ids, held, tile_ref, total):
    tiles, width, _ = total.shape
    for lane in range(GROUP):
        slot = g * GROUP + lane
        give = jnp.where(slot < count, ids[target, slot], tiles - 1)
        term = lax.dot_general(
            held[ids[source, slot]], tile_ref[slot], dims, preferred_element_type=jnp.float32
        )
        if term.shape[0] > width:
            term = term[:width] + term[width:]
        total[give] += term


def groups(source, target, dims, count, ids, held, tile_ref, total):
    def step(g, carry):
        group_of(g, source, target, dims, count, ids, held, tile_ref, total)
        return carry

    last = tile_ref.shape[0] // GROUP
    lax.fori_loop(0, jnp.minimum((count + GROUP - 1) // GROUP, last), step, 0)


def first_body(n_in, n_out, ids, live, place, *refs):
    pieces, tile_ref, outs = refs[:n_in], refs[n_in], refs[n_in + 1 : n_in + 1 + n_out]
    keep, held, total, sems = refs[n_in + 1 + n_out :]
    slots, side, _ = tile_ref.shape
    loads = []
    for g in range(slots // GROUP):
        span = pl.ds(g * GROUP, GROUP)
        loads.append(pltpu.make_async_copy(tile_ref.at[span], keep.at[span], sems.at[g]))
        loads[-1].start()
    collect(held, pieces, place[0], side)
    total[...] = jnp.zeros_like(total)
    count = live[0]
    for g in range(slots // GROUP):
        loads[g].wait()

        @pl.when(g * GROUP < count)
        def _():
            group_of(g, 1, 0, NT, count, ids, held, keep, total)

    emit(total, outs, place[1], side)


def back_body(n_in, ids, live, place, *refs):
    pieces, tile_ref, outs, (held, total) = refs[:n_in], refs[n_in], refs[n_in + 1 : -2], refs[-2:]
    side = tile_ref.shape[1]
    collect(held, pieces, place[1], side)
    total[...] = jnp.zeros_like(total)
    groups(0, 1, NN, live[0], ids, held, tile_ref, total)
    emit(total, outs, place[0], side)


def next_body(n_in, ids, live, place, *refs):
    pieces, (scale_ref, tile_ref, out_ref, spread, held, total) = refs[:n_in], refs[n_in:]
    tiles, width, side = out_ref.shape
    collect(spread, pieces, place[0], side)
    for tile in range(spread.shape[0]):
        value = spread[tile] * scale_ref[:, tile * side : (tile + 1) * side]
        high = value.astype(jnp.bfloat16)
        held[tile, :width] = high
        held[tile, width:] = (value - high.astype(jnp.float32)).astype(jnp.bfloat16)
    total[...] = jnp.zeros_like(total)
    groups(1, 0, NT, live[0], ids, held, tile_ref, total)
    out_ref[...] = total[:tiles]


def add(refs):
    total = refs[0][...].astype(jnp.float32)
    for ref in refs[1:]:
        total = total + ref[...].astype(jnp.float32)
    return total


def start_body(place, panel_ref, degree_ref, out_ref):
    share = panel_ref.shape[1]
    at = pl.multiple_of(place[0] * share, 128)
    scale = 1.0 / jnp.sqrt(degree_ref[:, pl.ds(at, share)].astype(jnp.float32))
    out_ref[...] = (panel_ref[...] * scale).astype(out_ref.dtype)


def query_body(*refs):
    part_refs, scale_ref, out_ref = refs[:-2], refs[-2], refs[-1]
    out_ref[...] = (add(part_refs) * scale_ref[...]).astype(out_ref.dtype)


def lift_body(*refs):
    part_refs, scale_ref, lifted_ref = refs[:-2], refs[-2], refs[-1]
    lifted_ref[...] = add(part_refs) * scale_ref[...]


def lift_gram_body(*refs):
    part_refs, scale_ref, lifted_ref, gram_ref = refs[:-3], refs[-3], refs[-2], refs[-1]
    lifted = add(part_refs) * scale_ref[...]
    lifted_ref[...] = lifted
    gram_ref[...] = lax.dot_general(lifted, lifted, NT, precision=HIGH, preferred_element_type=jnp.float32)


def gram_body(*refs):
    total = jnp.zeros(refs[-1].shape, jnp.float32)
    for ref in refs[:-1]:
        total = total + lax.dot_general(
            ref[...], ref[...], NT, precision=HIGH, preferred_element_type=jnp.float32
        )
    refs[-1][...] = total


def sum_body(*refs):
    refs[-1][...] = add(refs[:-1])


def apply_body(n_in, place, *refs):
    grams, total_ref, outs, done = refs[:n_in], refs[n_in], refs[n_in + 1 : -1], refs[-1]
    tiles, _, side = total_ref.shape
    inverse = inverse_factor(add(grams))
    for tile in range(tiles):
        done[tile] = lax.dot_general(
            inverse, total_ref[tile], NN, precision=HIGH, preferred_element_type=jnp.float32
        )
    emit(done, outs, place[1], side)


def finish_body(after, *refs):
    grams, lifted_ref, out_ref = refs[:-2], refs[-2], refs[-1]
    out_ref[...] = (
        lax.dot_general(
            inverse_factor(add(grams)), lifted_ref[...], NN, precision=HIGH, preferred_element_type=jnp.float32
        )
        * after
    )


def permute(value, axis, step):
    count = lax.axis_size(axis)
    return lax.ppermute(value, axis, [(i, (i + step) % count) for i in range(count)])


def spread_to(value, axis):
    return [value] + [permute(value, axis, step) for step in range(1, lax.axis_size(axis))]


def deal(values, axis):
    return [values[0]] + [permute(value, axis, step) for step, value in enumerate(values[1:], 1)]


def shards(tiles, tile_ids, tile_count, query_degree, product_degree, panel):
    tile_set = tiles[0, 0]
    ids = tile_ids[0, 0]
    live = tile_count[0]
    slots, side, _ = tile_set.shape
    width, share = panel.shape
    queries, products = query_degree.shape[0], product_degree.shape[0]
    query_tiles, product_tiles = queries // side, products // side
    n_row, n_col = lax.axis_size("row"), lax.axis_size("col")
    row_at, col_at = lax.axis_index("row"), lax.axis_index("col")
    place = jnp.stack([row_at, col_at]).astype(jnp.int32)
    columns = queries // n_col
    work = dict(flops=2 * slots * width * side * side, moved=2 * slots * side * side)
    scaled = call(start_body, "start", [SCALARS, WHOLE, WHOLE], bf16(width, share))(
        place, panel, product_degree[None, :]
    )
    pieces = spread_to(scaled, "row")
    my_pscale = 1.0 / jnp.sqrt(
        lax.dynamic_slice_in_dim(product_degree, row_at * share, share).astype(jnp.float32)
    )[None, :]
    my_qscale = 1.0 / jnp.sqrt(
        lax.dynamic_slice_in_dim(query_degree, col_at * columns, columns).astype(jnp.float32)
    )[None, :]
    pscale = 1.0 / jnp.sqrt(product_degree.astype(jnp.float32))[None, :]
    root_count = math.sqrt(products * n_col)
    sum_shapes = [f32(width, columns)] + [bf16(width, columns)] * (n_col - 1)
    query_scratch = pltpu.VMEM((query_tiles + 1, width, side), jnp.float32)
    product_scratch = pltpu.VMEM((product_tiles + 1, width, side), jnp.float32)
    for iteration in range(ITERS):
        if iteration == 0:
            *sums, tile_set = call(
                functools.partial(first_body, n_row, n_col),
                "forward",
                [SCALARS] * 3 + [WHOLE] * n_row + [AWAY],
                [*sum_shapes, bf16(slots, side, side)],
                [
                    pltpu.VMEM((product_tiles, width, side), jnp.bfloat16),
                    query_scratch,
                    pltpu.SemaphoreType.DMA((slots // GROUP,)),
                ],
                **work,
            )(ids, live, place, *pieces, tile_set)
        else:
            pieces = spread_to(lifted, "row")
            gram = call(gram_body, "gram", [WHOLE] * n_row, f32(width, width))(*pieces)
            grams = spread_to(gram, "col")
            total = call(
                functools.partial(next_body, n_row),
                "forward",
                [SCALARS] * 3 + [WHOLE] * (n_row + 2),
                f32(query_tiles, width, side),
                [
                    pltpu.VMEM((product_tiles, width, side), jnp.float32),
                    pltpu.VMEM((product_tiles, 2 * width, side), jnp.bfloat16),
                    query_scratch,
                ],
                **work,
            )(ids, live, place, *pieces, pscale, tile_set)
            sums = call(
                functools.partial(apply_body, n_col),
                "apply",
                [SCALARS] + [WHOLE] * (n_col + 1),
                sum_shapes,
                [pltpu.VMEM((query_tiles, width, side), jnp.float32)],
            )(place, *grams, total)
        parts = deal(sums, "col")
        rounded = call(query_body, "query", [WHOLE] * (n_col + 1), bf16(width, columns))(*parts, my_qscale)
        pieces = spread_to(rounded, "col")
        sums = call(
            functools.partial(back_body, n_col),
            "backward",
            [SCALARS] * 3 + [WHOLE] * (n_col + 1),
            [f32(width, share)] * n_row,
            [pltpu.VMEM((query_tiles, width, side), jnp.bfloat16), product_scratch],
            **work,
        )(ids, live, place, *pieces, tile_set)
        parts = deal(sums, "row")
        if iteration < ITERS - 1:
            lifted = call(lift_body, "lift", [WHOLE] * (n_row + 1), f32(width, share))(*parts, my_pscale)
    lifted, gram = call(
        lift_gram_body, "lift", [WHOLE] * (n_row + 1), [f32(width, share), f32(width, width)]
    )(*parts, my_pscale)
    gram = call(sum_body, "sum", [WHOLE] * n_row, f32(width, width))(*spread_to(gram, "row"))
    return call(
        functools.partial(finish_body, root_count), "finish", [WHOLE] * (n_col + 1), f32(width, share)
    )(*spread_to(gram, "col"), lifted)


def solution(mesh):
    in_specs = (
        P("row", "col", None, None, None),
        P("row", "col", None, None),
        P("row", "col"),
        P("row"),
        P("col"),
        P(None, ("col", "row")),
    )
    out_specs = P(None, ("col", "row"))
    return jax.shard_map(shards, mesh=mesh, in_specs=in_specs, out_specs=out_specs, check_vma=False)
```

time: 315 us -> 133 us (0.42)
  blocking collectives: 128 us -> 0 us
  waiting for transfers between devices: 107 us -> 30.8 us
  starting transfers between devices: 0.13 us -> 70.1 us
  matrix products: 28.4 us -> 0 us
  other arithmetic: 29.1 us -> 0.92 us
  Pallas kernels: 0 us -> 18.4 us
  between operations: 14 us -> 0.87 us
  local copies, waits for them, and re-layouts: 7.24 us -> 10.8 us
    reduce_scatter x4 -> x0, waiting for transfers between devices: 107 us -> none  [the longest x2 60.7 us: shards(): lax.psum_scatter(partial_sum, 'col', scatter_dimension=1, tiled=True)]
    psum x2 -> x0, blocking collectives: 79 us -> none  [shards(): lax.psum(jnp.einsum('ri,si->rs', lifted, lifted, precision=HIGH), ('row',...]
    ppermute x0 -> x57, starting transfers between devices: none -> 70.1 us  [permute(): lax.ppermute(value, axis, [(i, (i + step) % count) for i in range(count)])]
    all_gather x4 -> x0, blocking collectives: 49.1 us -> none  [the longest x2 28.4 us: shards(): query_block = lax.all_gather(rounded, 'col', axis=1, tiled=True)]
    ppermute x0 -> x57, waiting for transfers between devices: none -> 30.8 us  [permute(): lax.ppermute(value, axis, [(i, (i + step) % count) for i in range(count)])]
    dot_general x10 -> x0, matrix products: 25.3 us -> none  [the longest x2 7.18 us: shards(): jnp.einsum('rkj,kij->kri', picked, tile_set, preferred_element_type=jnp.f...]
    another operation x10 -> x1, other arithmetic: 24.1 us -> 0.07 us  [shards(): place = jnp.stack([row_at, col_at]).astype(jnp.int32)]
    pallas_call x0 -> x13, Pallas kernels: none -> 18.4 us  [the longest x1 3.93 us: shards(): call(functools.partial(apply_body, n_col), 'apply', [SCALARS] + [WHOLE] *...]
  transfers between devices with their start and end apart: 4 -> 57, of which waited for: 4 -> 25; matrix products, arithmetic and copies ran while one was open for 0% -> 1% of each run, Pallas kernels for 0% -> 2%
where the time goes in v2:
time: 133 us; the launch traced here: 132 us
  starting transfers between devices  70.1 us (53%)
  waiting for transfers between devices  30.8 us (23%)
  Pallas kernels  18.4 us (14%)
  local copies, waits for them, and re-layouts  10.8 us (8%)
    ppermute x57, starting transfers between devices, permute(): lax.ppermute(value, axis, [(i, (i + step) % count) for i in range(count)])  70.1 us
    ppermute x57, waiting for transfers between devices, permute(): lax.ppermute(value, axis, [(i, (i + step) % count) for i in range(count)])  30.8 us
    unnamed x20, local copies, waits for them, and re-layouts  10.8 us
    pallas_call x1, Pallas kernels, shards(): call(functools.partial(apply_body, n_col), 'apply', [SCALARS] + [WHOLE] *...  3.93 us
    pallas_call x2, Pallas kernels, shards(): call(functools.partial(back_body, n_col), 'backward', [SCALARS] * 3 + [WH...  3.77 us
    pallas_call x1, Pallas kernels, shards(): call(functools.partial(finish_body, root_count), 'finish', [WHOLE] * (n_c...  3.7 us
    pallas_call x1, Pallas kernels, shards(): call(functools.partial(first_body, n_row, n_col), 'forward', [SCALARS] *...  2.77 us
    pallas_call x1, Pallas kernels, shards(): call(functools.partial(next_body, n_row), 'forward', [SCALARS] * 3 + [WHO...  2.69 us
  transfers between devices with their start and end apart: 57, of which 25 were waited for; matrix products, arithmetic and copies ran while one was open for 1% of the time, Pallas kernels for 2%

profile of v2, /device:TPU:0, one launch (start us, length us, event | category | flops | bytes accessed | tf_op | source)
XLA Modules:
  0.0 131.9 jit_solution(16203339905384001248)
XLA Ops:
  2.3 3.0 %collective-permute-start = (bf16[64,512]{1,0:T(8,128)(2,1)S(1)}, bf16[64,512]{1,0:T(8,128)(2,1)S(1)}, u32[]{:S(2)}, u32[]{:S(2)}) collective-permute-start(bf16[64,512]{1,0:T(8,128)(2,1)S(1)} %start.1.refs_0_), channel_id=1, source_target_pairs={{0,8},{8,16},{16,24},{24,0},{1,9},{9,17},{17,25},{25,1},{2,10},{10... | collective-permute-start | bytes 196616 | tf_op jit(solution)/shard_map/ppermute | solution.py:251
  11.0 2.2 %copy-done.4 = bf16[1,1,32,256,256]{4,3,2,1,0:T(8,128)(2,1)S(1)} copy-done((bf16[1,1,32,256,256]{4,3,2,1,0:T(8,128)(2,1)S(1)}, bf16[1,1,32,256,256]{4,3,2,1,0:T(8,128)(2,1)}, u32[]{:S(2)}) %copy-start.4) | copy-done | bytes 4194328
  13.9 2.8 %forward.2 = (f32[64,256]{1,0:T(8,128)S(1)}, bf16[64,256]{1,0:T(8,128)(2,1)S(1)}, bf16[64,256]{1,0:T(8,128)(2,1)S(1)}, bf16[64,256]{1,0:T(8,128)(2,1)S(1)}, bf16...) custom-call(s32[2,32]{1,0:T(2,128)S(1)} %bitcast.18, ...), custom_call_target="tpu_custom_call" | custom-call | flops 268435456 | bytes 4194304 | tf_op jit(solution)/shard_map/forward/pallas_call | solution.py:292
  16.7 2.0 %copy-done = bf16[32,256,256]{2,1,0:T(8,128)(2,1)} copy-done((bf16[32,256,256]{2,1,0:T(8,128)(2,1)}, bf16[32,256,256]{2,1,0:T(8,128)(2,1)S(1)}, u32[]{:S(2)}) %copy-start) | copy-done | bytes 4194328
  19.4 3.0 %collective-permute-start.5 = (bf16[64,256]{1,0:T(8,128)(2,1)S(1)}, bf16[64,256]{1,0:T(8,128)(2,1)S(1)}, u32[]{:S(2)}, u32[]{:S(2)}) collective-permute-start(bf16[64,256]{1,0:T(8,128)(2,1)S(1)} %get-tuple-element.35), channel_id=1, source_target_pairs={{0,3},{1,4},{2,5},{3,6},{4,7},{5,0},{6,1},{7,2},{8,11},{9,12},{10,... | collective-permute-start | bytes 98312 | tf_op jit(solution)/shard_map/ppermute | solution.py:251
  32.2 1.7 %collective-permute-start.13 = (bf16[64,256]{1,0:T(8,128)(2,1)S(1)}, bf16[64,256]{1,0:T(8,128)(2,1)S(1)}, u32[]{:S(2)}, u32[]{:S(2)}) collective-permute-start(bf16[64,256]{1,0:T(8,128)(2,1)S(1)} %query.2.refs_0_), channel_id=1, source_target_pairs={{0,4},{1,5},{2,6},{3,7},{4,0},{5,1},{6,2},{7,3},{8,12},{9,13},{10,... | collective-permute-start | bytes 98312 | tf_op jit(solution)/shard_map/ppermute | solution.py:251
  33.8 1.8 %collective-permute-start.14 = (bf16[64,256]{1,0:T(8,128)(2,1)S(1)}, bf16[64,256]{1,0:T(8,128)(2,1)S(1)}, u32[]{:S(2)}, u32[]{:S(2)}) collective-permute-start(bf16[64,256]{1,0:T(8,128)(2,1)S(1)} %query.2.refs_0_), channel_id=1, source_target_pairs={{0,5},{1,6},{2,7},{3,0},{4,1},{5,2},{6,3},{7,4},{8,13},{9,14},{10,... | collective-permute-start | bytes 98312 | tf_op jit(solution)/shard_map/ppermute | solution.py:251
  37.7 1.9 %collective-permute-done.15.refs_6_ = bf16[64,256]{1,0:T(8,128)(2,1)S(1)} collective-permute-done((bf16[64,256]{1,0:T(8,128)(2,1)S(1)}, bf16[64,256]{1,0:T(8,128)(2,1)S(1)}, u32[]{:S(2)}, u32[]{:S(2)}) %collective-permute-start.15) | collective-permute-done | bytes 32800 | tf_op jit(solution)/shard_map/ppermute | solution.py:251
  39.7 2.2 %copy-done.1 = bf16[32,256,256]{2,1,0:T(8,128)(2,1)S(1)} copy-done((bf16[32,256,256]{2,1,0:T(8,128)(2,1)S(1)}, bf16[32,256,256]{2,1,0:T(8,128)(2,1)}, u32[]{:S(2)}) %copy-start.1) | copy-done | bytes 4194328
  41.8 1.9 %backward.2 = (f32[64,512]{1,0:T(8,128)S(1)}, f32[64,512]{1,0:T(8,128)S(1)}, f32[64,512]{1,0:T(8,128)S(1)}, f32[64,512]{1,0:T(8,128)S(1)}) custom-call(s32[2,32]{1,0:T(2,128)S(1)} %bitcast.19, s32[1]{0:T(128)} %bitcast.10.live, s32[2]{0:T(128)S(1)} %pad_add_fusion.place, bf16[64,256]{1,0:T(8,128)(2,1)S(1)} %query.2.refs_0_, ...), custom_call_target="tpu_custom_call" | custom-call | flops 268435456 | bytes 4194304 | tf_op jit(solution)/shard_map/backward/pallas_call | solution.py:330
  44.8 1.7 %collective-permute-start.18 = (f32[64,512]{1,0:T(8,128)S(1)}, f32[64,512]{1,0:T(8,128)S(1)}, u32[]{:S(2)}, u32[]{:S(2)}) collective-permute-start(f32[64,512]{1,0:T(8,128)S(1)} %get-tuple-element.43), channel_id=1, source_target_pairs={{0,16},{8,24},{16,0},{24,8},{1,17},{9,25},{17,1},{25,9},{2,18},{10... | collective-permute-start | bytes 393224 | tf_op jit(solution)/shard_map/ppermute | solution.py:251
  47.9 3.2 %collective-permute-done.17.refs_1_ = f32[64,512]{1,0:T(8,128)S(1)} collective-permute-done((f32[64,512]{1,0:T(8,128)S(1)}, f32[64,512]{1,0:T(8,128)S(1)}, u32[]{:S(2)}, u32[]{:S(2)}) %collective-permute-start.17) | collective-permute-done | bytes 131104 | tf_op jit(solution)/shard_map/ppermute | solution.py:251
  51.1 2.0 %collective-permute-done.18.refs_2_ = f32[64,512]{1,0:T(8,128)S(1)} collective-permute-done((f32[64,512]{1,0:T(8,128)S(1)}, f32[64,512]{1,0:T(8,128)S(1)}, u32[]{:S(2)}, u32[]{:S(2)}) %collective-permute-start.18) | collective-permute-done | bytes 131104 | tf_op jit(solution)/shard_map/ppermute | solution.py:251
  53.2 1.8 %collective-permute-start.20 = (f32[64,512]{1,0:T(8,128)S(1)}, f32[64,512]{1,0:T(8,128)S(1)}, u32[]{:S(2)}, u32[]{:S(2)}) collective-permute-start(f32[64,512]{1,0:T(8,128)S(1)} %lift.2.refs_0_), channel_id=1, source_target_pairs={{0,8},{8,16},{16,24},{24,0},{1,9},{9,17},{17,25},{25,1},{2,10},{10... | collective-permute-start | bytes 393224 | tf_op jit(solution)/shard_map/ppermute | solution.py:251
  55.6 1.9 %collective-permute-start.22 = (f32[64,512]{1,0:T(8,128)S(1)}, f32[64,512]{1,0:T(8,128)S(1)}, u32[]{:S(2)}, u32[]{:S(2)}) collective-permute-start(f32[64,512]{1,0:T(8,128)S(1)} %lift.2.refs_0_), channel_id=1, source_target_pairs={{0,24},{8,0},{16,8},{24,16},{1,25},{9,1},{17,9},{25,17},{2,26},{10... | collective-permute-start | bytes 393224 | tf_op jit(solution)/shard_map/ppermute | solution.py:251
  57.5 3.0 %collective-permute-done.20.refs_1_ = f32[64,512]{1,0:T(8,128)S(1)} collective-permute-done((f32[64,512]{1,0:T(8,128)S(1)}, f32[64,512]{1,0:T(8,128)S(1)}, u32[]{:S(2)}, u32[]{:S(2)}) %collective-permute-start.20) | collective-permute-done | bytes 131104 | tf_op jit(solution)/shard_map/ppermute | solution.py:251
  60.5 1.9 %collective-permute-done.21.refs_2_ = f32[64,512]{1,0:T(8,128)S(1)} collective-permute-done((f32[64,512]{1,0:T(8,128)S(1)}, f32[64,512]{1,0:T(8,128)S(1)}, u32[]{:S(2)}, u32[]{:S(2)}) %collective-permute-start.21) | collective-permute-done | bytes 131104 | tf_op jit(solution)/shard_map/ppermute | solution.py:251
  65.8 2.3 %collective-permute-start.26 = (f32[64,64]{1,0:T(8,128)S(1)}, f32[64,64]{1,0:T(8,128)S(1)}, u32[]{:S(2)}, u32[]{:S(2)}) collective-permute-start(f32[64,64]{1,0:T(8,128)S(1)} %gram.1.refs_0_), channel_id=1, source_target_pairs={{0,4},{1,5},{2,6},{3,7},{4,0},{5,1},{6,2},{7,3},{8,12},{9,13},{10,... | collective-permute-start | bytes 49160 | tf_op jit(solution)/shard_map/ppermute | solution.py:251
  68.2 2.0 %collective-permute-start.28 = (f32[64,64]{1,0:T(8,128)S(1)}, f32[64,64]{1,0:T(8,128)S(1)}, u32[]{:S(2)}, u32[]{:S(2)}) collective-permute-start(f32[64,64]{1,0:T(8,128)S(1)} %gram.1.refs_0_), channel_id=1, source_target_pairs={{0,6},{1,7},{2,0},{3,1},{4,2},{5,3},{6,4},{7,5},{8,14},{9,15},{10,... | collective-permute-start | bytes 49160 | tf_op jit(solution)/shard_map/ppermute | solution.py:251
  70.8 2.2 %copy-done.2 = bf16[32,256,256]{2,1,0:T(8,128)(2,1)S(1)} copy-done((bf16[32,256,256]{2,1,0:T(8,128)(2,1)S(1)}, bf16[32,256,256]{2,1,0:T(8,128)(2,1)}, u32[]{:S(2)}) %copy-start.2) | copy-done | bytes 4194328
  73.0 2.7 %forward.3.refs_8_ = f32[8,64,256]{2,1,0:T(8,128)S(1)} custom-call(s32[2,32]{1,0:T(2,128)S(1)} %bitcast.20, s32[1]{0:T(128)} %bitcast.11.live, s32[2]{0:T(128)S(1)} %pad_add_fusion.place, f32[64,512]{1,0:T(8,128)S(1)} %lift.2.refs_0_, f32[64,512]{1,0:T(8,128)S(1)} %collective-permute-done.20.refs_1_, f32[64,512]{1,0:T(8,128)S(1)} %collective-permute-done.21.refs_2_, ...), custom_call_target="tpu_custom_call" | custom-call | flops 268435456 | bytes 4194304 | tf_op jit(solution)/shard_map/forward/pallas_call | solution.py:308
  75.8 3.9 %apply.1 = (f32[64,256]{1,0:T(8,128)S(1)}, bf16[64,256]{1,0:T(8,128)(2,1)S(1)}, bf16[64,256]{1,0:T(8,128)(2,1)S(1)}, bf16[64,256]{1,0:T(8,128)(2,1)S(1)}, bf16[6...) custom-call(s32[2]{0:T(128)S(1)} %pad_add_fusion.place, ...), custom_call_target="tpu_custom_call" | custom-call | tf_op jit(solution)/shard_map/apply/pallas_call | solution.py:320
  81.5 2.3 %collective-permute-start.33 = (bf16[64,256]{1,0:T(8,128)(2,1)S(1)}, bf16[64,256]{1,0:T(8,128)(2,1)S(1)}, u32[]{:S(2)}, u32[]{:S(2)}) collective-permute-start(bf16[64,256]{1,0:T(8,128)(2,1)S(1)} %get-tuple-element.49), channel_id=1, source_target_pairs={{0,4},{1,5},{2,6},{3,7},{4,0},{5,1},{6,2},{7,3},{8,12},{9,13},{10,... | collective-permute-start | bytes 98312 | tf_op jit(solution)/shard_map/ppermute | solution.py:251
  90.1 1.7 %collective-permute-start.38 = (bf16[64,256]{1,0:T(8,128)(2,1)S(1)}, bf16[64,256]{1,0:T(8,128)(2,1)S(1)}, u32[]{:S(2)}, u32[]{:S(2)}) collective-permute-start(bf16[64,256]{1,0:T(8,128)(2,1)S(1)} %query.3.refs_0_), channel_id=1, source_target_pairs={{0,2},{1,3},{2,4},{3,5},{4,6},{5,7},{6,0},{7,1},{8,10},{9,11},{10,... | collective-permute-start | bytes 98312 | tf_op jit(solution)/shard_map/ppermute | solution.py:251
  100.1 1.9 %backward.3 = (f32[64,512]{1,0:T(8,128)S(1)}, f32[64,512]{1,0:T(8,128)S(1)}, f32[64,512]{1,0:T(8,128)S(1)}, f32[64,512]{1,0:T(8,128)S(1)}) custom-call(s32[2,32]{1,0:T(2,128)S(1)} %bitcast.21, s32[1]{0:T(128)} %bitcast.12.live, s32[2]{0:T(128)S(1)} %pad_add_fusion.place, bf16[64,256]{1,0:T(8,128)(2,1)S(1)} %query.3.refs_0_, ...), custom_call_target="tpu_custom_call" | custom-call | flops 268435456 | bytes 4194304 | tf_op jit(solution)/shard_map/backward/pallas_call | solution.py:330
  103.9 2.2 %collective-permute-start.46 = (f32[64,512]{1,0:T(8,128)S(1)}, f32[64,512]{1,0:T(8,128)S(1)}, u32[]{:S(2)}, u32[]{:S(2)}) collective-permute-start(f32[64,512]{1,0:T(8,128)S(1)} %get-tuple-element.56), channel_id=1, source_target_pairs={{0,24},{8,0},{16,8},{24,16},{1,25},{9,1},{17,9},{25,17},{2,26},{10... | collective-permute-start | bytes 393224 | tf_op jit(solution)/shard_map/ppermute | solution.py:251
  106.1 2.7 %collective-permute-done.44.refs_1_ = f32[64,512]{1,0:T(8,128)S(1)} collective-permute-done((f32[64,512]{1,0:T(8,128)S(1)}, f32[64,512]{1,0:T(8,128)S(1)}, u32[]{:S(2)}, u32[]{:S(2)}) %collective-permute-start.44) | collective-permute-done | bytes 131104 | tf_op jit(solution)/shard_map/ppermute | solution.py:251
  108.7 2.0 %collective-permute-done.45.refs_2_ = f32[64,512]{1,0:T(8,128)S(1)} collective-permute-done((f32[64,512]{1,0:T(8,128)S(1)}, f32[64,512]{1,0:T(8,128)S(1)}, u32[]{:S(2)}, u32[]{:S(2)}) %collective-permute-start.45) | collective-permute-done | bytes 131104 | tf_op jit(solution)/shard_map/ppermute | solution.py:251
  111.6 1.8 %collective-permute-start.47 = (f32[64,64]{1,0:T(8,128)S(1)}, f32[64,64]{1,0:T(8,128)S(1)}, u32[]{:S(2)}, u32[]{:S(2)}) collective-permute-start(f32[64,64]{1,0:T(8,128)S(1)} %get-tuple-element.57.refs_0_), channel_id=1, source_target_pairs={{0,8},{8,16},{16,24},{24,0},{1,9},{9,17},{17,25},{25,1},{2,10},{10... | collective-permute-start | bytes 49160 | tf_op jit(solution)/shard_map/ppermute | solution.py:251
  113.7 2.0 %collective-permute-start.49 = (f32[64,64]{1,0:T(8,128)S(1)}, f32[64,64]{1,0:T(8,128)S(1)}, u32[]{:S(2)}, u32[]{:S(2)}) collective-permute-start(f32[64,64]{1,0:T(8,128)S(1)} %get-tuple-element.57.refs_0_), channel_id=1, source_target_pairs={{0,24},{8,0},{16,8},{24,16},{1,25},{9,1},{17,9},{25,17},{2,26},{10... | collective-permute-start | bytes 49160 | tf_op jit(solution)/shard_map/ppermute | solution.py:251
  118.8 2.7 %collective-permute-start.52 = (f32[64,64]{1,0:T(8,128)S(1)}, f32[64,64]{1,0:T(8,128)S(1)}, u32[]{:S(2)}, u32[]{:S(2)}) collective-permute-start(f32[64,64]{1,0:T(8,128)S(1)} %sum.1.refs_0_), channel_id=1, source_target_pairs={{0,3},{1,4},{2,5},{3,6},{4,7},{5,0},{6,1},{7,2},{8,11},{9,12},{10,... | collective-permute-start | bytes 49160 | tf_op jit(solution)/shard_map/ppermute | solution.py:251
  128.2 3.7 %finish.1 = f32[64,512]{1,0:T(8,128)} custom-call(f32[64,64]{1,0:T(8,128)S(1)} %sum.1.refs_0_, f32[64,64]{1,0:T(8,128)S(1)} %collective-permute-done.50.refs_1_, f32[64,64]{1,0:T(8,128)S(1)} %collective-permute-done.51.refs_2_, f32[64,64]{1,0:T(8,128)S(1)} %collective-permute-done.52.refs_3_, f32[64,64]{1,0:T(8,128)S(1)} %collective-permute-done.53.refs_4_, ...), custom_call_target="tpu_custom_call" | custom-call | tf_op jit(solution)/shard_map/finish/pallas_call | solution.py:345
  (119 shorter events, 57.2 us)
Async XLA Ops:
  2.3 6.6 %collective-permute-start = (bf16[64,512]{1,0:T(8,128)(2,1)S(1)}, bf16[64,512]{1,0:T(8,128)(2,1)S(1)}, u32[]{:S(2)}, u32[]{:S(2)}) collective-permute-start(bf16[64,512]{1,0:T(8,128)(2,1)S(1)} %start.1.refs_0_), channel_id=1, source_target_pairs={{0,8},{8,16},{16,24},{24,0},{1,9},{9,17},{17,25},{25,1},{2,10},{10... | collective-permute-start | bytes 196616 | tf_op jit(solution)/shard_map/ppermute | solution.py:251
  18.7 6.1 %collective-permute-start.3 = (bf16[64,256]{1,0:T(8,128)(2,1)S(1)}, bf16[64,256]{1,0:T(8,128)(2,1)S(1)}, u32[]{:S(2)}, u32[]{:S(2)}) collective-permute-start(bf16[64,256]{1,0:T(8,128)(2,1)S(1)} %get-tuple-element.33), channel_id=1, source_target_pairs={{0,1},{1,2},{2,3},{3,4},{4,5},{5,6},{6,7},{7,0},{8,9},{9,10},{10,1... | collective-permute-start | bytes 98312 | tf_op jit(solution)/shard_map/ppermute | solution.py:251
  18.7 7.0 %collective-permute-start.4 = (bf16[64,256]{1,0:T(8,128)(2,1)S(1)}, bf16[64,256]{1,0:T(8,128)(2,1)S(1)}, u32[]{:S(2)}, u32[]{:S(2)}) collective-permute-start(bf16[64,256]{1,0:T(8,128)(2,1)S(1)} %get-tuple-element.34), channel_id=1, source_target_pairs={{0,2},{1,3},{2,4},{3,5},{4,6},{5,7},{6,0},{7,1},{8,10},{9,11},{10,... | collective-permute-start | bytes 98312 | tf_op jit(solution)/shard_map/ppermute | solution.py:251
  19.4 8.5 %collective-permute-start.5 = (bf16[64,256]{1,0:T(8,128)(2,1)S(1)}, bf16[64,256]{1,0:T(8,128)(2,1)S(1)}, u32[]{:S(2)}, u32[]{:S(2)}) collective-permute-start(bf16[64,256]{1,0:T(8,128)(2,1)S(1)} %get-tuple-element.35), channel_id=1, source_target_pairs={{0,3},{1,4},{2,5},{3,6},{4,7},{5,0},{6,1},{7,2},{8,11},{9,12},{10,... | collective-permute-start | bytes 98312 | tf_op jit(solution)/shard_map/ppermute | solution.py:251
  29.2 6.4 %collective-permute-start.10 = (bf16[64,256]{1,0:T(8,128)(2,1)S(1)}, bf16[64,256]{1,0:T(8,128)(2,1)S(1)}, u32[]{:S(2)}, u32[]{:S(2)}) collective-permute-start(bf16[64,256]{1,0:T(8,128)(2,1)S(1)} %query.2.refs_0_), channel_id=1, source_target_pairs={{0,1},{1,2},{2,3},{3,4},{4,5},{5,6},{6,7},{7,0},{8,9},{9,10},{10,1... | collective-permute-start | bytes 98312 | tf_op jit(solution)/shard_map/ppermute | solution.py:251
  30.1 6.5 %collective-permute-start.11 = (bf16[64,256]{1,0:T(8,128)(2,1)S(1)}, bf16[64,256]{1,0:T(8,128)(2,1)S(1)}, u32[]{:S(2)}, u32[]{:S(2)}) collective-permute-start(bf16[64,256]{1,0:T(8,128)(2,1)S(1)} %query.2.refs_0_), channel_id=1, source_target_pairs={{0,2},{1,3},{2,4},{3,5},{4,6},{5,7},{6,0},{7,1},{8,10},{9,11},{10,... | collective-permute-start | bytes 98312 | tf_op jit(solution)/shard_map/ppermute | solution.py:251
  30.7 6.2 %collective-permute-start.12 = (bf16[64,256]{1,0:T(8,128)(2,1)S(1)}, bf16[64,256]{1,0:T(8,128)(2,1)S(1)}, u32[]{:S(2)}, u32[]{:S(2)}) collective-permute-start(bf16[64,256]{1,0:T(8,128)(2,1)S(1)} %query.2.refs_0_), channel_id=1, source_target_pairs={{0,3},{1,4},{2,5},{3,6},{4,7},{5,0},{6,1},{7,2},{8,11},{9,12},{10,... | collective-permute-start | bytes 98312 | tf_op jit(solution)/shard_map/ppermute | solution.py:251
  43.8 7.3 %collective-permute-start.17 = (f32[64,512]{1,0:T(8,128)S(1)}, f32[64,512]{1,0:T(8,128)S(1)}, u32[]{:S(2)}, u32[]{:S(2)}) collective-permute-start(f32[64,512]{1,0:T(8,128)S(1)} %get-tuple-element.42), channel_id=1, source_target_pairs={{0,8},{8,16},{16,24},{24,0},{1,9},{9,17},{17,25},{25,1},{2,10},{10... | collective-permute-start | bytes 393224 | tf_op jit(solution)/shard_map/ppermute | solution.py:251
  44.8 8.3 %collective-permute-start.18 = (f32[64,512]{1,0:T(8,128)S(1)}, f32[64,512]{1,0:T(8,128)S(1)}, u32[]{:S(2)}, u32[]{:S(2)}) collective-permute-start(f32[64,512]{1,0:T(8,128)S(1)} %get-tuple-element.43), channel_id=1, source_target_pairs={{0,16},{8,24},{16,0},{24,8},{1,17},{9,25},{17,1},{25,9},{2,18},{10... | collective-permute-start | bytes 393224 | tf_op jit(solution)/shard_map/ppermute | solution.py:251
  46.5 6.6 %collective-permute-start.19 = (f32[64,512]{1,0:T(8,128)S(1)}, f32[64,512]{1,0:T(8,128)S(1)}, u32[]{:S(2)}, u32[]{:S(2)}) collective-permute-start(f32[64,512]{1,0:T(8,128)S(1)} %get-tuple-element.44), channel_id=1, source_target_pairs={{0,24},{8,0},{16,8},{24,16},{1,25},{9,1},{17,9},{25,17},{2,26},{10... | collective-permute-start | bytes 393224 | tf_op jit(solution)/shard_map/ppermute | solution.py:251
  53.2 7.3 %collective-permute-start.20 = (f32[64,512]{1,0:T(8,128)S(1)}, f32[64,512]{1,0:T(8,128)S(1)}, u32[]{:S(2)}, u32[]{:S(2)}) collective-permute-start(f32[64,512]{1,0:T(8,128)S(1)} %lift.2.refs_0_), channel_id=1, source_target_pairs={{0,8},{8,16},{16,24},{24,0},{1,9},{9,17},{17,25},{25,1},{2,10},{10... | collective-permute-start | bytes 393224 | tf_op jit(solution)/shard_map/ppermute | solution.py:251
  54.9 7.4 %collective-permute-start.21 = (f32[64,512]{1,0:T(8,128)S(1)}, f32[64,512]{1,0:T(8,128)S(1)}, u32[]{:S(2)}, u32[]{:S(2)}) collective-permute-start(f32[64,512]{1,0:T(8,128)S(1)} %lift.2.refs_0_), channel_id=1, source_target_pairs={{0,16},{8,24},{16,0},{24,8},{1,17},{9,25},{17,1},{25,9},{2,18},{10... | collective-permute-start | bytes 393224 | tf_op jit(solution)/shard_map/ppermute | solution.py:251
  55.6 6.8 %collective-permute-start.22 = (f32[64,512]{1,0:T(8,128)S(1)}, f32[64,512]{1,0:T(8,128)S(1)}, u32[]{:S(2)}, u32[]{:S(2)}) collective-permute-start(f32[64,512]{1,0:T(8,128)S(1)} %lift.2.refs_0_), channel_id=1, source_target_pairs={{0,24},{8,0},{16,8},{24,16},{1,25},{9,1},{17,9},{25,17},{2,26},{10... | collective-permute-start | bytes 393224 | tf_op jit(solution)/shard_map/ppermute | solution.py:251
  63.0 7.2 %collective-permute-start.24 = (f32[64,64]{1,0:T(8,128)S(1)}, f32[64,64]{1,0:T(8,128)S(1)}, u32[]{:S(2)}, u32[]{:S(2)}) collective-permute-start(f32[64,64]{1,0:T(8,128)S(1)} %gram.1.refs_0_), channel_id=1, source_target_pairs={{0,2},{1,3},{2,4},{3,5},{4,6},{5,7},{6,0},{7,1},{8,10},{9,11},{10,... | collective-permute-start | bytes 49160 | tf_op jit(solution)/shard_map/ppermute | solution.py:251
  64.3 11.4 %collective-permute-start.25 = (f32[64,64]{1,0:T(8,128)S(1)}, f32[64,64]{1,0:T(8,128)S(1)}, u32[]{:S(2)}, u32[]{:S(2)}) collective-permute-start(f32[64,64]{1,0:T(8,128)S(1)} %gram.1.refs_0_), channel_id=1, source_target_pairs={{0,3},{1,4},{2,5},{3,6},{4,7},{5,0},{6,1},{7,2},{8,11},{9,12},{10,... | collective-permute-start | bytes 49160 | tf_op jit(solution)/shard_map/ppermute | solution.py:251
  65.8 9.9 %collective-permute-start.26 = (f32[64,64]{1,0:T(8,128)S(1)}, f32[64,64]{1,0:T(8,128)S(1)}, u32[]{:S(2)}, u32[]{:S(2)}) collective-permute-start(f32[64,64]{1,0:T(8,128)S(1)} %gram.1.refs_0_), channel_id=1, source_target_pairs={{0,4},{1,5},{2,6},{3,7},{4,0},{5,1},{6,2},{7,3},{8,12},{9,13},{10,... | collective-permute-start | bytes 49160 | tf_op jit(solution)/shard_map/ppermute | solution.py:251
  68.1 7.6 %collective-permute-start.27 = (f32[64,64]{1,0:T(8,128)S(1)}, f32[64,64]{1,0:T(8,128)S(1)}, u32[]{:S(2)}, u32[]{:S(2)}) collective-permute-start(f32[64,64]{1,0:T(8,128)S(1)} %gram.1.refs_0_), channel_id=1, source_target_pairs={{0,5},{1,6},{2,7},{3,0},{4,1},{5,2},{6,3},{7,4},{8,13},{9,14},{10,... | collective-permute-start | bytes 49160 | tf_op jit(solution)/shard_map/ppermute | solution.py:251
  68.2 7.5 %collective-permute-start.28 = (f32[64,64]{1,0:T(8,128)S(1)}, f32[64,64]{1,0:T(8,128)S(1)}, u32[]{:S(2)}, u32[]{:S(2)}) collective-permute-start(f32[64,64]{1,0:T(8,128)S(1)} %gram.1.refs_0_), channel_id=1, source_target_pairs={{0,6},{1,7},{2,0},{3,1},{4,2},{5,3},{6,4},{7,5},{8,14},{9,15},{10,... | collective-permute-start | bytes 49160 | tf_op jit(solution)/shard_map/ppermute | solution.py:251
  79.8 6.8 %collective-permute-start.31 = (bf16[64,256]{1,0:T(8,128)(2,1)S(1)}, bf16[64,256]{1,0:T(8,128)(2,1)S(1)}, u32[]{:S(2)}, u32[]{:S(2)}) collective-permute-start(bf16[64,256]{1,0:T(8,128)(2,1)S(1)} %get-tuple-element.47), channel_id=1, source_target_pairs={{0,2},{1,3},{2,4},{3,5},{4,6},{5,7},{6,0},{7,1},{8,10},{9,11},{10,... | collective-permute-start | bytes 98312 | tf_op jit(solution)/shard_map/ppermute | solution.py:251
  80.1 7.4 %collective-permute-start.32 = (bf16[64,256]{1,0:T(8,128)(2,1)S(1)}, bf16[64,256]{1,0:T(8,128)(2,1)S(1)}, u32[]{:S(2)}, u32[]{:S(2)}) collective-permute-start(bf16[64,256]{1,0:T(8,128)(2,1)S(1)} %get-tuple-element.48), channel_id=1, source_target_pairs={{0,3},{1,4},{2,5},{3,6},{4,7},{5,0},{6,1},{7,2},{8,11},{9,12},{10,... | collective-permute-start | bytes 98312 | tf_op jit(solution)/shard_map/ppermute | solution.py:251
  81.5 5.9 %collective-permute-start.33 = (bf16[64,256]{1,0:T(8,128)(2,1)S(1)}, bf16[64,256]{1,0:T(8,128)(2,1)S(1)}, u32[]{:S(2)}, u32[]{:S(2)}) collective-permute-start(bf16[64,256]{1,0:T(8,128)(2,1)S(1)} %get-tuple-element.49), channel_id=1, source_target_pairs={{0,4},{1,5},{2,6},{3,7},{4,0},{5,1},{6,2},{7,3},{8,12},{9,13},{10,... | collective-permute-start | bytes 98312 | tf_op jit(solution)/shard_map/ppermute | solution.py:251
  89.1 6.9 %collective-permute-start.37 = (bf16[64,256]{1,0:T(8,128)(2,1)S(1)}, bf16[64,256]{1,0:T(8,128)(2,1)S(1)}, u32[]{:S(2)}, u32[]{:S(2)}) collective-permute-start(bf16[64,256]{1,0:T(8,128)(2,1)S(1)} %query.3.refs_0_), channel_id=1, source_target_pairs={{0,1},{1,2},{2,3},{3,4},{4,5},{5,6},{6,7},{7,0},{8,9},{9,10},{10,1... | collective-permute-start | bytes 98312 | tf_op jit(solution)/shard_map/ppermute | solution.py:251
  90.1 6.5 %collective-permute-start.38 = (bf16[64,256]{1,0:T(8,128)(2,1)S(1)}, bf16[64,256]{1,0:T(8,128)(2,1)S(1)}, u32[]{:S(2)}, u32[]{:S(2)}) collective-permute-start(bf16[64,256]{1,0:T(8,128)(2,1)S(1)} %query.3.refs_0_), channel_id=1, source_target_pairs={{0,2},{1,3},{2,4},{3,5},{4,6},{5,7},{6,0},{7,1},{8,10},{9,11},{10,... | collective-permute-start | bytes 98312 | tf_op jit(solution)/shard_map/ppermute | solution.py:251
  91.8 6.2 %collective-permute-start.39 = (bf16[64,256]{1,0:T(8,128)(2,1)S(1)}, bf16[64,256]{1,0:T(8,128)(2,1)S(1)}, u32[]{:S(2)}, u32[]{:S(2)}) collective-permute-start(bf16[64,256]{1,0:T(8,128)(2,1)S(1)} %query.3.refs_0_), channel_id=1, source_target_pairs={{0,3},{1,4},{2,5},{3,6},{4,7},{5,0},{6,1},{7,2},{8,11},{9,12},{10,... | collective-permute-start | bytes 98312 | tf_op jit(solution)/shard_map/ppermute | solution.py:251
  93.0 6.2 %collective-permute-start.40 = (bf16[64,256]{1,0:T(8,128)(2,1)S(1)}, bf16[64,256]{1,0:T(8,128)(2,1)S(1)}, u32[]{:S(2)}, u32[]{:S(2)}) collective-permute-start(bf16[64,256]{1,0:T(8,128)(2,1)S(1)} %query.3.refs_0_), channel_id=1, source_target_pairs={{0,4},{1,5},{2,6},{3,7},{4,0},{5,1},{6,2},{7,3},{8,12},{9,13},{10,... | collective-permute-start | bytes 98312 | tf_op jit(solution)/shard_map/ppermute | solution.py:251
  102.0 6.7 %collective-permute-start.44 = (f32[64,512]{1,0:T(8,128)S(1)}, f32[64,512]{1,0:T(8,128)S(1)}, u32[]{:S(2)}, u32[]{:S(2)}) collective-permute-start(f32[64,512]{1,0:T(8,128)S(1)} %get-tuple-element.54), channel_id=1, source_target_pairs={{0,8},{8,16},{16,24},{24,0},{1,9},{9,17},{17,25},{25,1},{2,10},{10... | collective-permute-start | bytes 393224 | tf_op jit(solution)/shard_map/ppermute | solution.py:251
  103.2 7.5 %collective-permute-start.45 = (f32[64,512]{1,0:T(8,128)S(1)}, f32[64,512]{1,0:T(8,128)S(1)}, u32[]{:S(2)}, u32[]{:S(2)}) collective-permute-start(f32[64,512]{1,0:T(8,128)S(1)} %get-tuple-element.55), channel_id=1, source_target_pairs={{0,16},{8,24},{16,0},{24,8},{1,17},{9,25},{17,1},{25,9},{2,18},{10... | collective-permute-start | bytes 393224 | tf_op jit(solution)/shard_map/ppermute | solution.py:251
  103.9 7.5 %collective-permute-start.46 = (f32[64,512]{1,0:T(8,128)S(1)}, f32[64,512]{1,0:T(8,128)S(1)}, u32[]{:S(2)}, u32[]{:S(2)}) collective-permute-start(f32[64,512]{1,0:T(8,128)S(1)} %get-tuple-element.56), channel_id=1, source_target_pairs={{0,24},{8,0},{16,8},{24,16},{1,25},{9,1},{17,9},{25,17},{2,26},{10... | collective-permute-start | bytes 393224 | tf_op jit(solution)/shard_map/ppermute | solution.py:251
  117.6 6.3 %collective-permute-start.50 = (f32[64,64]{1,0:T(8,128)S(1)}, f32[64,64]{1,0:T(8,128)S(1)}, u32[]{:S(2)}, u32[]{:S(2)}) collective-permute-start(f32[64,64]{1,0:T(8,128)S(1)} %sum.1.refs_0_), channel_id=1, source_target_pairs={{0,1},{1,2},{2,3},{3,4},{4,5},{5,6},{6,7},{7,0},{8,9},{9,10},{10,1... | collective-permute-start | bytes 49160 | tf_op jit(solution)/shard_map/ppermute | solution.py:251
  117.6 7.0 %collective-permute-start.51 = (f32[64,64]{1,0:T(8,128)S(1)}, f32[64,64]{1,0:T(8,128)S(1)}, u32[]{:S(2)}, u32[]{:S(2)}) collective-permute-start(f32[64,64]{1,0:T(8,128)S(1)} %sum.1.refs_0_), channel_id=1, source_target_pairs={{0,2},{1,3},{2,4},{3,5},{4,6},{5,7},{6,0},{7,1},{8,10},{9,11},{10,... | collective-permute-start | bytes 49160 | tf_op jit(solution)/shard_map/ppermute | solution.py:251
  118.8 6.9 %collective-permute-start.52 = (f32[64,64]{1,0:T(8,128)S(1)}, f32[64,64]{1,0:T(8,128)S(1)}, u32[]{:S(2)}, u32[]{:S(2)}) collective-permute-start(f32[64,64]{1,0:T(8,128)S(1)} %sum.1.refs_0_), channel_id=1, source_target_pairs={{0,3},{1,4},{2,5},{3,6},{4,7},{5,0},{6,1},{7,2},{8,11},{9,12},{10,... | collective-permute-start | bytes 49160 | tf_op jit(solution)/shard_map/ppermute | solution.py:251
  121.4 5.8 %collective-permute-start.53 = (f32[64,64]{1,0:T(8,128)S(1)}, f32[64,64]{1,0:T(8,128)S(1)}, u32[]{:S(2)}, u32[]{:S(2)}) collective-permute-start(f32[64,64]{1,0:T(8,128)S(1)} %sum.1.refs_0_), channel_id=1, source_target_pairs={{0,4},{1,5},{2,6},{3,7},{4,0},{5,1},{6,2},{7,3},{8,12},{9,13},{10,... | collective-permute-start | bytes 49160 | tf_op jit(solution)/shard_map/ppermute | solution.py:251
  (35 other events, 219.0 us)

commit v3 on v2

--- a/solution.py
+++ b/solution.py
@@ -12,7 +12,7 @@
 GROUP = 8
 PANEL_STEP = 4
 HIGH = lax.Precision.HIGHEST
-VMEM_BYTES = 40 * 1024 * 1024
+VMEM_BYTES = 12 * 1024 * 1024
 NT = (((1,), (1,)), ((), ()))
 NN = (((1,), (0,)), ((), ()))
 
@@ -47,7 +47,7 @@
 
 WHOLE = pl.BlockSpec(memory_space=pltpu.VMEM)
 SCALARS = pl.BlockSpec(memory_space=pltpu.SMEM)
-AWAY = pl.BlockSpec(memory_space=pl.ANY)
+AWAY = pl.BlockSpec(memory_space=pltpu.MemorySpace.HBM)
 
 
 def call(body, name, in_specs, out_shape, scratch=(), flops=0, moved=0):
@@ -64,6 +64,10 @@
     )
 
 
+def in_hbm(value):
+    return pltpu.with_memory_space_constraint(value, pltpu.MemorySpace.HBM)
+
+
 def f32(*shape):
     return jax.ShapeDtypeStruct(shape, jnp.float32)
 
@@ -103,15 +107,30 @@
 
 
 def emit(total, out_refs, me, side):
-    count = len(out_refs)
     for step, out_ref in enumerate(out_refs):
-        get(total, lax.rem(me + step, count), out_ref, side)
+        get(total, lax.rem(me + step, len(out_refs)), out_ref, side)
+
+
+def emit_pairs(total, mine_ref, other_ref, me, side):
+    chips = mine_ref.shape[0]
+    for step in range(chips):
+        chip = lax.rem(me // 2 + step, chips)
+        get(total, 2 * chip + me % 2, mine_ref.at[step], side)
+        get(total, 2 * chip + 1 - me % 2, other_ref.at[step], side)
 
 
 def collect(held, piece_refs, me, side):
     count = len(piece_refs)
     for step, piece_ref in enumerate(piece_refs):
         put(held, lax.rem(me + count - step, count), piece_ref[...], side)
+
+
+def collect_pairs(held, mine_ref, other_ref, me, side):
+    chips = mine_ref.shape[0]
+    for step in range(chips):
+        chip = lax.rem(me // 2 + chips - step, chips)
+        put(held, 2 * chip + me % 2, mine_ref[step], side)
+        put(held, 2 * chip + 1 - me % 2, other_ref[step], side)
 
 
 def group_of(g, source, target, dims, count, ids, held, tile_ref, total):
@@ -136,9 +155,8 @@
     lax.fori_loop(0, jnp.minimum((count + GROUP - 1) // GROUP, last), step, 0)
 
 
-def first_body(n_in, n_out, ids, live, place, *refs):
-    pieces, tile_ref, outs = refs[:n_in], refs[n_in], refs[n_in + 1 : n_in + 1 + n_out]
-    keep, held, total, sems = refs[n_in + 1 + n_out :]
+def first_body(n_in, ids, live, place, *refs):
+    pieces, (tile_ref, mine_ref, other_ref, keep, held, total, sems) = refs[:n_in], refs[n_in:]
     slots, side, _ = tile_ref.shape
     loads = []
     for g in range(slots // GROUP):
@@ -155,16 +173,16 @@
         def _():
             group_of(g, 1, 0, NT, count, ids, held, keep, total)
 
-    emit(total, outs, place[1], side)
-
-
-def back_body(n_in, ids, live, place, *refs):
-    pieces, tile_ref, outs, (held, total) = refs[:n_in], refs[n_in], refs[n_in + 1 : -2], refs[-2:]
+    emit_pairs(total, mine_ref, other_ref, place[1], side)
+
+
+def back_body(ids, live, place, here_ref, there_ref, tile_ref, *refs):
+    out_refs, (held, total) = refs[:-2], refs[-2:]
     side = tile_ref.shape[1]
-    collect(held, pieces, place[1], side)
+    collect_pairs(held, here_ref, there_ref, place[1], side)
     total[...] = jnp.zeros_like(total)
     groups(0, 1, NN, live[0], ids, held, tile_ref, total)
-    emit(total, outs, place[0], side)
+    emit(total, out_refs, place[0], side)
 
 
 def next_body(n_in, ids, live, place, *refs):
@@ -188,11 +206,47 @@
     return total
 
 
-def start_body(place, panel_ref, degree_ref, out_ref):
+def start_body(place, panel_ref, degree_ref, out_ref, held, degrees, sems):
     share = panel_ref.shape[1]
     at = pl.multiple_of(place[0] * share, 128)
-    scale = 1.0 / jnp.sqrt(degree_ref[:, pl.ds(at, share)].astype(jnp.float32))
-    out_ref[...] = (panel_ref[...] * scale).astype(out_ref.dtype)
+    loads = [
+        pltpu.make_async_copy(degree_ref, degrees, sems.at[0]),
+        pltpu.make_async_copy(panel_ref, held, sems.at[1]),
+    ]
+    for load in loads:
+        load.start()
+    for load in loads:
+        load.wait()
+    scale = 1.0 / jnp.sqrt(degrees[:, pl.ds(at, share)].astype(jnp.float32))
+    out_ref[...] = (held[...] * scale).astype(out_ref.dtype)
+
+
+def scales_body(place, product_ref, query_ref, my_product_ref, product_out, my_query_ref):
+    product_out[...] = 1.0 / jnp.sqrt(product_ref[...].astype(jnp.float32))
+    share = my_product_ref.shape[1]
+    at = pl.multiple_of(place[0] * share, 128)
+    my_product_ref[...] = product_out[:, pl.ds(at, share)]
+    columns = my_query_ref.shape[1]
+    if columns % 128 == 0:
+        at = pl.multiple_of(place[1] * columns, 128)
+        my_query_ref[...] = 1.0 / jnp.sqrt(query_ref[:, pl.ds(at, columns)].astype(jnp.float32))
+    else:
+        for step in range(query_ref.shape[1] // columns):
+
+            @pl.when(place[1] == step)
+            def _():
+                degree = query_ref[:, step * columns : (step + 1) * columns]
+                my_query_ref[...] = 1.0 / jnp.sqrt(degree.astype(jnp.float32))
+
+
+def pair_body(mine_ref, got_ref, *outs):
+    for step, out_ref in enumerate(outs):
+        out_ref[...] = (mine_ref[step] + got_ref[step]).astype(out_ref.dtype)
+
+
+def join_body(*refs):
+    for step, ref in enumerate(refs[:-1]):
+        refs[-1][step] = ref[...]
 
 
 def query_body(*refs):
@@ -226,14 +280,14 @@
 
 
 def apply_body(n_in, place, *refs):
-    grams, total_ref, outs, done = refs[:n_in], refs[n_in], refs[n_in + 1 : -1], refs[-1]
+    grams, (total_ref, mine_ref, other_ref, done) = refs[:n_in], refs[n_in:]
     tiles, _, side = total_ref.shape
     inverse = inverse_factor(add(grams))
     for tile in range(tiles):
         done[tile] = lax.dot_general(
             inverse, total_ref[tile], NN, precision=HIGH, preferred_element_type=jnp.float32
         )
-    emit(done, outs, place[1], side)
+    emit_pairs(done, mine_ref, other_ref, place[1], side)
 
 
 def finish_body(after, *refs):
@@ -251,12 +305,24 @@
     return lax.ppermute(value, axis, [(i, (i + step) % count) for i in range(count)])
 
 
-def spread_to(value, axis):
-    return [value] + [permute(value, axis, step) for step in range(1, lax.axis_size(axis))]
-
-
-def deal(values, axis):
-    return [values[0]] + [permute(value, axis, step) for step, value in enumerate(values[1:], 1)]
+def swap(value):
+    return lax.ppermute(value, "col", [(i, i ^ 1) for i in range(lax.axis_size("col"))])
+
+
+def spread_to(value, axis, stride=1):
+    return [value] + [permute(value, axis, step) for step in range(stride, lax.axis_size(axis), stride)]
+
+
+def deal(values, axis, stride=1):
+    return [values[0]] + [permute(value, axis, step * stride) for step, value in enumerate(values[1:], 1)]
+
+
+def gram_over_col(gram):
+    return spread_to(add_up(gram, swap(gram)), "col", 2)
+
+
+def add_up(*values):
+    return call(sum_body, "sum", [WHOLE] * len(values), f32(*values[0].shape))(*values)
 
 
 def shards(tiles, tile_ids, tile_count, query_degree, product_degree, panel):
@@ -268,43 +334,48 @@
     queries, products = query_degree.shape[0], product_degree.shape[0]
     query_tiles, product_tiles = queries // side, products // side
     n_row, n_col = lax.axis_size("row"), lax.axis_size("col")
-    row_at, col_at = lax.axis_index("row"), lax.axis_index("col")
-    place = jnp.stack([row_at, col_at]).astype(jnp.int32)
+    chips = n_col // 2
+    place = jnp.stack([lax.axis_index("row"), lax.axis_index("col")]).astype(jnp.int32)
     columns = queries // n_col
     work = dict(flops=2 * slots * width * side * side, moved=2 * slots * side * side)
-    scaled = call(start_body, "start", [SCALARS, WHOLE, WHOLE], bf16(width, share))(
-        place, panel, product_degree[None, :]
-    )
+    scaled = call(
+        start_body,
+        "start",
+        [SCALARS, AWAY, AWAY],
+        bf16(width, share),
+        [
+            pltpu.VMEM((width, share), jnp.float32),
+            pltpu.VMEM((1, products), jnp.int32),
+            pltpu.SemaphoreType.DMA((2,)),
+        ],
+    )(place, in_hbm(panel), in_hbm(product_degree[None, :]))
     pieces = spread_to(scaled, "row")
-    my_pscale = 1.0 / jnp.sqrt(
-        lax.dynamic_slice_in_dim(product_degree, row_at * share, share).astype(jnp.float32)
-    )[None, :]
-    my_qscale = 1.0 / jnp.sqrt(
-        lax.dynamic_slice_in_dim(query_degree, col_at * columns, columns).astype(jnp.float32)
-    )[None, :]
-    pscale = 1.0 / jnp.sqrt(product_degree.astype(jnp.float32))[None, :]
+    my_pscale, pscale, my_qscale = call(
+        scales_body, "scales", [SCALARS, WHOLE, WHOLE], [f32(1, share), f32(1, products), f32(1, columns)]
+    )(place, product_degree[None, :], query_degree[None, :])
     root_count = math.sqrt(products * n_col)
-    sum_shapes = [f32(width, columns)] + [bf16(width, columns)] * (n_col - 1)
+    half_shapes = [f32(chips, width, columns)] * 2
     query_scratch = pltpu.VMEM((query_tiles + 1, width, side), jnp.float32)
     product_scratch = pltpu.VMEM((product_tiles + 1, width, side), jnp.float32)
     for iteration in range(ITERS):
         if iteration == 0:
-            *sums, tile_set = call(
-                functools.partial(first_body, n_row, n_col),
+            mine, other, tile_set = call(
+                functools.partial(first_body, n_row),
                 "forward",
                 [SCALARS] * 3 + [WHOLE] * n_row + [AWAY],
-                [*sum_shapes, bf16(slots, side, side)],
+                [*half_shapes, pltpu.VMEM((slots, side, side), jnp.bfloat16)],
                 [
                     pltpu.VMEM((product_tiles, width, side), jnp.bfloat16),
                     query_scratch,
                     pltpu.SemaphoreType.DMA((slots // GROUP,)),
                 ],
                 **work,
-            )(ids, live, place, *pieces, tile_set)
+            )(ids, live, place, *pieces, in_hbm(tile_set))
+            tile_set = pltpu.with_memory_space_constraint(tile_set, pltpu.VMEM)
         else:
             pieces = spread_to(lifted, "row")
             gram = call(gram_body, "gram", [WHOLE] * n_row, f32(width, width))(*pieces)
-            grams = spread_to(gram, "col")
+            grams = gram_over_col(gram)
             total = call(
                 functools.partial(next_body, n_row),
                 "forward",
@@ -317,34 +388,39 @@
                 ],
                 **work,
             )(ids, live, place, *pieces, pscale, tile_set)
-            sums = call(
-                functools.partial(apply_body, n_col),
+            mine, other = call(
+                functools.partial(apply_body, chips),
                 "apply",
-                [SCALARS] + [WHOLE] * (n_col + 1),
-                sum_shapes,
+                [SCALARS] + [WHOLE] * (chips + 1),
+                half_shapes,
                 [pltpu.VMEM((query_tiles, width, side), jnp.float32)],
             )(place, *grams, total)
-        parts = deal(sums, "col")
-        rounded = call(query_body, "query", [WHOLE] * (n_col + 1), bf16(width, columns))(*parts, my_qscale)
-        pieces = spread_to(rounded, "col")
         sums = call(
-            functools.partial(back_body, n_col),
+            pair_body, "pair", [WHOLE] * 2, [f32(width, columns)] + [bf16(width, columns)] * (chips - 1)
+        )(mine, swap(other))
+        parts = deal(sums, "col", 2)
+        rounded = call(query_body, "query", [WHOLE] * (chips + 1), bf16(width, columns))(*parts, my_qscale)
+        here = call(join_body, "join", [WHOLE] * chips, bf16(chips, width, columns))(
+            *spread_to(rounded, "col", 2)
+        )
+        sums = call(
+            back_body,
             "backward",
-            [SCALARS] * 3 + [WHOLE] * (n_col + 1),
+            [SCALARS] * 3 + [WHOLE] * 3,
             [f32(width, share)] * n_row,
             [pltpu.VMEM((query_tiles, width, side), jnp.bfloat16), product_scratch],
             **work,
-        )(ids, live, place, *pieces, tile_set)
+        )(ids, live, place, here, swap(here), tile_set)
         parts = deal(sums, "row")
         if iteration < ITERS - 1:
             lifted = call(lift_body, "lift", [WHOLE] * (n_row + 1), f32(width, share))(*parts, my_pscale)
     lifted, gram = call(
         lift_gram_body, "lift", [WHOLE] * (n_row + 1), [f32(width, share), f32(width, width)]
     )(*parts, my_pscale)
-    gram = call(sum_body, "sum", [WHOLE] * n_row, f32(width, width))(*spread_to(gram, "row"))
+    grams = gram_over_col(add_up(*spread_to(gram, "row")))
     return call(
-        functools.partial(finish_body, root_count), "finish", [WHOLE] * (n_col + 1), f32(width, share)
-    )(*spread_to(gram, "col"), lifted)
+        functools.partial(finish_body, root_count), "finish", [WHOLE] * (chips + 1), f32(width, share)
+    )(*grams, lifted)
 
 
 def solution(mesh):

time: 133 us -> 118 us (0.89)
  starting transfers between devices: 70.1 us -> 43.3 us
  waiting for transfers between devices: 30.8 us -> 52.6 us
  local copies, waits for them, and re-layouts: 10.8 us -> 0.69 us
  Pallas kernels: 18.4 us -> 20.8 us
    ppermute x57 -> x33, starting transfers between devices: 70.1 us -> 42.8 us  [permute(): lax.ppermute(value, axis, [(i, (i + step) % count) for i in range(count)])]
    ppermute x57 -> x33, waiting for transfers between devices: 30.8 us -> 44.5 us  [permute(): lax.ppermute(value, axis, [(i, (i + step) % count) for i in range(count)])]
    unnamed x20 -> x8, local copies, waits for them, and re-layouts: 10.8 us -> 0.69 us
    ppermute x0 -> x6, waiting for transfers between devices: none -> 8.1 us  [swap(): lax.ppermute(value, 'col', [(i, i ^ 1) for i in range(lax.axis_size('col'...]
    pallas_call x9 -> x16, Pallas kernels: 14.8 us -> 17.2 us  [the longest x1 3.92 us: shards(): call(functools.partial(apply_body, chips), 'apply', [SCALARS] + [WHOLE] *...]
  transfers between devices with their start and end apart: 57 -> 39, of which waited for: 25 -> 35; matrix products, arithmetic and copies ran while one was open for 1% -> 0% of each run, Pallas kernels for 2% -> 3%
where the time goes in v3:
time: 118 us
  waiting for transfers between devices  52.6 us (45%)
  starting transfers between devices  43.3 us (37%)
  Pallas kernels  20.8 us (18%)
    ppermute x33, waiting for transfers between devices, permute(): lax.ppermute(value, axis, [(i, (i + step) % count) for i in range(count)])  44.5 us
    ppermute x33, starting transfers between devices, permute(): lax.ppermute(value, axis, [(i, (i + step) % count) for i in range(count)])  42.8 us
    ppermute x6, waiting for transfers between devices, swap(): lax.ppermute(value, 'col', [(i, i ^ 1) for i in range(lax.axis_size('col'...  8.1 us
    pallas_call x1, Pallas kernels, shards(): call(functools.partial(apply_body, chips), 'apply', [SCALARS] + [WHOLE] *...  3.92 us
    pallas_call x2, Pallas kernels, shards(): call(back_body, 'backward', [SCALARS] * 3 + [WHOLE] * 3, [f32(width, shar...  3.74 us
    pallas_call x1, Pallas kernels, shards(): call(functools.partial(finish_body, root_count), 'finish', [WHOLE] * (chi...  3.7 us
    pallas_call x1, Pallas kernels, shards(): call(functools.partial(first_body, n_row), 'forward', [SCALARS] * 3 + [WH...  3.65 us
    pallas_call x1, Pallas kernels, shards(): call(functools.partial(next_body, n_row), 'forward', [SCALARS] * 3 + [WHO...  2.67 us
  transfers between devices with their start and end apart: 39, of which 35 were waited for; matrix products, arithmetic and copies ran while one was open for 0% of the time, Pallas kernels for 3%

profile of v3, /device:TPU:0, one launch (start us, length us, event | category | flops | bytes accessed | tf_op | source)
XLA Modules:
  0.0 118.2 jit_solution(6853660208388643435)
XLA Ops:
  1.6 4.0 %collective-permute-start.2 = (bf16[64,512]{1,0:T(8,128)(2,1)S(1)}, bf16[64,512]{1,0:T(8,128)(2,1)S(1)}, u32[]{:S(2)}, u32[]{:S(2)}) collective-permute-start(bf16[64,512]{1,0:T(8,128)(2,1)S(1)} %start.1.refs_0_), channel_id=1, source_target_pairs={{0,24},{8,0},{16,8},{24,16},{1,25},{9,1},{17,9},{25,17},{2,26},{10... | collective-permute-start | bytes 196616 | tf_op jit(solution)/shard_map/ppermute | solution.py:305
  7.6 2.6 %collective-permute-done.1.refs_2_ = bf16[64,512]{1,0:T(8,128)(2,1)S(1)} collective-permute-done((bf16[64,512]{1,0:T(8,128)(2,1)S(1)}, bf16[64,512]{1,0:T(8,128)(2,1)S(1)}, u32[]{:S(2)}, u32[]{:S(2)}) %collective-permute-start.1) | collective-permute-done | bytes 65568 | tf_op jit(solution)/shard_map/ppermute | solution.py:305
  11.9 3.6 %forward.2 = (f32[4,64,256]{2,1,0:T(8,128)S(1)}, f32[4,64,256]{2,1,0:T(8,128)S(1)}, bf16[32,256,256]{2,1,0:T(8,128)(2,1)S(1)}) custom-call(s32[2,32]{1,0:T(2,128)S(1)} %bitcast.13, s32[1]{0:T(128)} %bitcast.7.live, s32[2]{0:T(128)S(1)} %pad_add_fusion.place, bf16[64,512]{1,0:T(8,128)(2,1)S(1)} %start.1.refs_0_, ...), custom_call_target="tpu_custom_call" | custom-call | flops 268435456 | bytes 4194304 | tf_op jit(solution)/shard_map/forward/pallas_call | solution.py:362
  15.6 1.5 %collective-permute-done.3.got_ref = f32[4,64,256]{2,1,0:T(8,128)S(1)} collective-permute-done((f32[4,64,256]{2,1,0:T(8,128)S(1)}, f32[4,64,256]{2,1,0:T(8,128)S(1)}, u32[]{:S(2)}, u32[]{:S(2)}) %collective-permute-start.3) | collective-permute-done | bytes 262176 | tf_op jit(solution)/shard_map/ppermute | solution.py:309
  18.4 3.0 %collective-permute-start.5 = (bf16[64,256]{1,0:T(8,128)(2,1)S(1)}, bf16[64,256]{1,0:T(8,128)(2,1)S(1)}, u32[]{:S(2)}, u32[]{:S(2)}) collective-permute-start(bf16[64,256]{1,0:T(8,128)(2,1)S(1)} %get-tuple-element.35), channel_id=1, source_target_pairs={{0,4},{1,5},{2,6},{3,7},{4,0},{5,1},{6,2},{7,3},{8,12},{9,13},{10,... | collective-permute-start | bytes 98312 | tf_op jit(solution)/shard_map/ppermute | solution.py:305
  25.4 2.3 %collective-permute-start.9 = (bf16[64,256]{1,0:T(8,128)(2,1)S(1)}, bf16[64,256]{1,0:T(8,128)(2,1)S(1)}, u32[]{:S(2)}, u32[]{:S(2)}) collective-permute-start(bf16[64,256]{1,0:T(8,128)(2,1)S(1)} %query.2.refs_0_), channel_id=1, source_target_pairs={{0,6},{1,7},{2,0},{3,1},{4,2},{5,3},{6,4},{7,5},{8,14},{9,15},{10,... | collective-permute-start | bytes 98312 | tf_op jit(solution)/shard_map/ppermute | solution.py:305
  29.3 3.2 %collective-permute-done.8.refs_2_ = bf16[64,256]{1,0:T(8,128)(2,1)S(1)} collective-permute-done((bf16[64,256]{1,0:T(8,128)(2,1)S(1)}, bf16[64,256]{1,0:T(8,128)(2,1)S(1)}, u32[]{:S(2)}, u32[]{:S(2)}) %collective-permute-start.8) | collective-permute-done | bytes 32800 | tf_op jit(solution)/shard_map/ppermute | solution.py:305
  34.9 1.9 %backward.2 = (f32[64,512]{1,0:T(8,128)S(1)}, f32[64,512]{1,0:T(8,128)S(1)}, f32[64,512]{1,0:T(8,128)S(1)}, f32[64,512]{1,0:T(8,128)S(1)}) custom-call(s32[2,32]{1,0:T(2,128)S(1)} %bitcast.14, s32[1]{0:T(128)} %bitcast.8.live, s32[2]{0:T(128)S(1)} %pad_add_fusion.place, bf16[4,64,256]{2,1,0:T(8,128)(2,1)S(1)} %join.2.here_ref, ...), custom_call_target="tpu_custom_call" | custom-call | flops 268435456 | bytes 4194304 | tf_op jit(solution)/shard_map/backward/pallas_call | solution.py:406
  36.9 1.6 %collective-permute-start.12 = (f32[64,512]{1,0:T(8,128)S(1)}, f32[64,512]{1,0:T(8,128)S(1)}, u32[]{:S(2)}, u32[]{:S(2)}) collective-permute-start(f32[64,512]{1,0:T(8,128)S(1)} %get-tuple-element.41), channel_id=1, source_target_pairs={{0,16},{8,24},{16,0},{24,8},{1,17},{9,25},{17,1},{25,9},{2,18},{10... | collective-permute-start | bytes 393224 | tf_op jit(solution)/shard_map/ppermute | solution.py:305
  38.5 2.8 %collective-permute-start.13 = (f32[64,512]{1,0:T(8,128)S(1)}, f32[64,512]{1,0:T(8,128)S(1)}, u32[]{:S(2)}, u32[]{:S(2)}) collective-permute-start(f32[64,512]{1,0:T(8,128)S(1)} %get-tuple-element.42), channel_id=1, source_target_pairs={{0,24},{8,0},{16,8},{24,16},{1,25},{9,1},{17,9},{25,17},{2,26},{10... | collective-permute-start | bytes 393224 | tf_op jit(solution)/shard_map/ppermute | solution.py:305
  41.3 2.5 %collective-permute-done.11.refs_1_ = f32[64,512]{1,0:T(8,128)S(1)} collective-permute-done((f32[64,512]{1,0:T(8,128)S(1)}, f32[64,512]{1,0:T(8,128)S(1)}, u32[]{:S(2)}, u32[]{:S(2)}) %collective-permute-start.11) | collective-permute-done | bytes 131104 | tf_op jit(solution)/shard_map/ppermute | solution.py:305
  46.0 1.6 %collective-permute-start.16 = (f32[64,512]{1,0:T(8,128)S(1)}, f32[64,512]{1,0:T(8,128)S(1)}, u32[]{:S(2)}, u32[]{:S(2)}) collective-permute-start(f32[64,512]{1,0:T(8,128)S(1)} %lift.2.refs_0_), channel_id=1, source_target_pairs={{0,24},{8,0},{16,8},{24,16},{1,25},{9,1},{17,9},{25,17},{2,26},{10... | collective-permute-start | bytes 393224 | tf_op jit(solution)/shard_map/ppermute | solution.py:305
  47.6 1.6 %collective-permute-start.15 = (f32[64,512]{1,0:T(8,128)S(1)}, f32[64,512]{1,0:T(8,128)S(1)}, u32[]{:S(2)}, u32[]{:S(2)}) collective-permute-start(f32[64,512]{1,0:T(8,128)S(1)} %lift.2.refs_0_), channel_id=1, source_target_pairs={{0,16},{8,24},{16,0},{24,8},{1,17},{9,25},{17,1},{25,9},{2,18},{10... | collective-permute-start | bytes 393224 | tf_op jit(solution)/shard_map/ppermute | solution.py:305
  49.2 3.0 %collective-permute-done.16.refs_3_ = f32[64,512]{1,0:T(8,128)S(1)} collective-permute-done((f32[64,512]{1,0:T(8,128)S(1)}, f32[64,512]{1,0:T(8,128)S(1)}, u32[]{:S(2)}, u32[]{:S(2)}) %collective-permute-start.16) | collective-permute-done | bytes 131104 | tf_op jit(solution)/shard_map/ppermute | solution.py:305
  52.2 3.1 %collective-permute-done.15.refs_2_ = f32[64,512]{1,0:T(8,128)S(1)} collective-permute-done((f32[64,512]{1,0:T(8,128)S(1)}, f32[64,512]{1,0:T(8,128)S(1)}, u32[]{:S(2)}, u32[]{:S(2)}) %collective-permute-start.15) | collective-permute-done | bytes 131104 | tf_op jit(solution)/shard_map/ppermute | solution.py:305
  58.9 2.0 %collective-permute-start.18 = (f32[64,64]{1,0:T(8,128)S(1)}, f32[64,64]{1,0:T(8,128)S(1)}, u32[]{:S(2)}, u32[]{:S(2)}) collective-permute-start(f32[64,64]{1,0:T(8,128)S(1)} %sum.3.refs_0_), channel_id=1, source_target_pairs={{0,2},{1,3},{2,4},{3,5},{4,6},{5,7},{6,0},{7,1},{8,10},{9,11},{10,... | collective-permute-start | bytes 49160 | tf_op jit(solution)/shard_map/ppermute | solution.py:305
  60.9 2.7 %forward.3.refs_4_ = f32[8,64,256]{2,1,0:T(8,128)S(1)} custom-call(s32[2,32]{1,0:T(2,128)S(1)} %bitcast.15, s32[1]{0:T(128)} %bitcast.9.live, s32[2]{0:T(128)S(1)} %pad_add_fusion.place, f32[64,512]{1,0:T(8,128)S(1)} %lift.2.refs_0_, f32[64,512]{1,0:T(8,128)S(1)} %collective-permute-done.14.refs_1_, f32[64,512]{1,0:T(8,128)S(1)} %collective-permute-done.15.refs_2_, ...), custom_call_target="tpu_custom_call" | custom-call | flops 268435456 | bytes 4194304 | tf_op jit(solution)/shard_map/forward/pallas_call | solution.py:379
  64.6 3.9 %apply.1 = (f32[4,64,256]{2,1,0:T(8,128)S(1)}, f32[4,64,256]{2,1,0:T(8,128)S(1)}) custom-call(s32[2]{0:T(128)S(1)} %pad_add_fusion.place, f32[64,64]{1,0:T(8,128)S(1)} %sum.3.refs_0_, f32[64,64]{1,0:T(8,128)S(1)} %collective-permute-done.18.refs_1_, f32[64,64]{1,0:T(8,128)S(1)} %collective-permute-done.19.refs_2_, ...), custom_call_target="tpu_custom_call" | custom-call | tf_op jit(solution)/shard_map/apply/pallas_call | solution.py:391
  71.8 2.3 %collective-permute-start.24 = (bf16[64,256]{1,0:T(8,128)(2,1)S(1)}, bf16[64,256]{1,0:T(8,128)(2,1)S(1)}, u32[]{:S(2)}, u32[]{:S(2)}) collective-permute-start(bf16[64,256]{1,0:T(8,128)(2,1)S(1)} %get-tuple-element.50), channel_id=1, source_target_pairs={{0,6},{1,7},{2,0},{3,1},{4,2},{5,3},{6,4},{7,5},{8,14},{9,15},{10,... | collective-permute-start | bytes 98312 | tf_op jit(solution)/shard_map/ppermute | solution.py:305
  74.1 2.1 %collective-permute-done.22.refs_1_ = bf16[64,256]{1,0:T(8,128)(2,1)S(1)} collective-permute-done((bf16[64,256]{1,0:T(8,128)(2,1)S(1)}, bf16[64,256]{1,0:T(8,128)(2,1)S(1)}, u32[]{:S(2)}, u32[]{:S(2)}) %collective-permute-start.22) | collective-permute-done | bytes 32800 | tf_op jit(solution)/shard_map/ppermute | solution.py:305
  76.5 3.3 %collective-permute-start.27 = (bf16[64,256]{1,0:T(8,128)(2,1)S(1)}, bf16[64,256]{1,0:T(8,128)(2,1)S(1)}, u32[]{:S(2)}, u32[]{:S(2)}) collective-permute-start(bf16[64,256]{1,0:T(8,128)(2,1)S(1)} %query.3.refs_0_), channel_id=1, source_target_pairs={{0,6},{1,7},{2,0},{3,1},{4,2},{5,3},{6,4},{7,5},{8,14},{9,15},{10,... | collective-permute-start | bytes 98312 | tf_op jit(solution)/shard_map/ppermute | solution.py:305
  81.4 3.2 %collective-permute-done.26.refs_2_ = bf16[64,256]{1,0:T(8,128)(2,1)S(1)} collective-permute-done((bf16[64,256]{1,0:T(8,128)(2,1)S(1)}, bf16[64,256]{1,0:T(8,128)(2,1)S(1)}, u32[]{:S(2)}, u32[]{:S(2)}) %collective-permute-start.26) | collective-permute-done | bytes 32800 | tf_op jit(solution)/shard_map/ppermute | solution.py:305
  87.2 1.9 %backward.3 = (f32[64,512]{1,0:T(8,128)S(1)}, f32[64,512]{1,0:T(8,128)S(1)}, f32[64,512]{1,0:T(8,128)S(1)}, f32[64,512]{1,0:T(8,128)S(1)}) custom-call(s32[2,32]{1,0:T(2,128)S(1)} %bitcast.16, s32[1]{0:T(128)} %bitcast.10.live, s32[2]{0:T(128)S(1)} %pad_add_fusion.place, bf16[4,64,256]{2,1,0:T(8,128)(2,1)S(1)} %join.3.here_ref, ...), custom_call_target="tpu_custom_call" | custom-call | flops 268435456 | bytes 4194304 | tf_op jit(solution)/shard_map/backward/pallas_call | solution.py:406
  90.4 2.6 %collective-permute-start.31 = (f32[64,512]{1,0:T(8,128)S(1)}, f32[64,512]{1,0:T(8,128)S(1)}, u32[]{:S(2)}, u32[]{:S(2)}) collective-permute-start(f32[64,512]{1,0:T(8,128)S(1)} %get-tuple-element.54), channel_id=1, source_target_pairs={{0,24},{8,0},{16,8},{24,16},{1,25},{9,1},{17,9},{25,17},{2,26},{10... | collective-permute-start | bytes 393224 | tf_op jit(solution)/shard_map/ppermute | solution.py:305
  93.0 3.2 %collective-permute-done.29.refs_1_ = f32[64,512]{1,0:T(8,128)S(1)} collective-permute-done((f32[64,512]{1,0:T(8,128)S(1)}, f32[64,512]{1,0:T(8,128)S(1)}, u32[]{:S(2)}, u32[]{:S(2)}) %collective-permute-start.29) | collective-permute-done | bytes 131104 | tf_op jit(solution)/shard_map/ppermute | solution.py:305
  97.9 2.3 %collective-permute-start.34 = (f32[64,64]{1,0:T(8,128)S(1)}, f32[64,64]{1,0:T(8,128)S(1)}, u32[]{:S(2)}, u32[]{:S(2)}) collective-permute-start(f32[64,64]{1,0:T(8,128)S(1)} %get-tuple-element.55.refs_0_), channel_id=1, source_target_pairs={{0,24},{8,0},{16,8},{24,16},{1,25},{9,1},{17,9},{25,17},{2,26},{10... | collective-permute-start | bytes 49160 | tf_op jit(solution)/shard_map/ppermute | solution.py:305
  102.1 2.0 %collective-permute-done.33.refs_2_ = f32[64,64]{1,0:T(8,128)S(1)} collective-permute-done((f32[64,64]{1,0:T(8,128)S(1)}, f32[64,64]{1,0:T(8,128)S(1)}, u32[]{:S(2)}, u32[]{:S(2)}) %collective-permute-start.33) | collective-permute-done | bytes 16416 | tf_op jit(solution)/shard_map/ppermute | solution.py:305
  104.1 1.8 %collective-permute-done.32.refs_1_ = f32[64,64]{1,0:T(8,128)S(1)} collective-permute-done((f32[64,64]{1,0:T(8,128)S(1)}, f32[64,64]{1,0:T(8,128)S(1)}, u32[]{:S(2)}, u32[]{:S(2)}) %collective-permute-start.32) | collective-permute-done | bytes 16416 | tf_op jit(solution)/shard_map/ppermute | solution.py:305
  108.8 2.0 %collective-permute-start.36 = (f32[64,64]{1,0:T(8,128)S(1)}, f32[64,64]{1,0:T(8,128)S(1)}, u32[]{:S(2)}, u32[]{:S(2)}) collective-permute-start(f32[64,64]{1,0:T(8,128)S(1)} %sum.5.refs_0_), channel_id=1, source_target_pairs={{0,2},{1,3},{2,4},{3,5},{4,6},{5,7},{6,0},{7,1},{8,10},{9,11},{10,... | collective-permute-start | bytes 49160 | tf_op jit(solution)/shard_map/ppermute | solution.py:305
  111.2 1.7 %collective-permute-done.37.refs_2_ = f32[64,64]{1,0:T(8,128)S(1)} collective-permute-done((f32[64,64]{1,0:T(8,128)S(1)}, f32[64,64]{1,0:T(8,128)S(1)}, u32[]{:S(2)}, u32[]{:S(2)}) %collective-permute-start.37) | collective-permute-done | bytes 16416 | tf_op jit(solution)/shard_map/ppermute | solution.py:305
  112.8 1.7 %collective-permute-done.36.refs_1_ = f32[64,64]{1,0:T(8,128)S(1)} collective-permute-done((f32[64,64]{1,0:T(8,128)S(1)}, f32[64,64]{1,0:T(8,128)S(1)}, u32[]{:S(2)}, u32[]{:S(2)}) %collective-permute-start.36) | collective-permute-done | bytes 16416 | tf_op jit(solution)/shard_map/ppermute | solution.py:305
  114.5 3.7 %finish.1 = f32[64,512]{1,0:T(8,128)} custom-call(f32[64,64]{1,0:T(8,128)S(1)} %sum.5.refs_0_, f32[64,64]{1,0:T(8,128)S(1)} %collective-permute-done.36.refs_1_, f32[64,64]{1,0:T(8,128)S(1)} %collective-permute-done.37.refs_2_, f32[64,64]{1,0:T(8,128)S(1)} %collective-permute-done.38.refs_3_, f32[64,512]{1,0:T(8,128)S(1)} %get-tuple-element.56.refs_4_), custom_call_target="tpu_custom_call" | custom-call | tf_op jit(solution)/shard_map/finish/pallas_call | solution.py:421
  (75 shorter events, 36.8 us)
Async XLA Ops:
  1.6 6.0 %collective-permute-start.2 = (bf16[64,512]{1,0:T(8,128)(2,1)S(1)}, bf16[64,512]{1,0:T(8,128)(2,1)S(1)}, u32[]{:S(2)}, u32[]{:S(2)}) collective-permute-start(bf16[64,512]{1,0:T(8,128)(2,1)S(1)} %start.1.refs_0_), channel_id=1, source_target_pairs={{0,24},{8,0},{16,8},{24,16},{1,25},{9,1},{17,9},{25,17},{2,26},{10... | collective-permute-start | bytes 196616 | tf_op jit(solution)/shard_map/ppermute | solution.py:305
  5.5 4.7 %collective-permute-start.1 = (bf16[64,512]{1,0:T(8,128)(2,1)S(1)}, bf16[64,512]{1,0:T(8,128)(2,1)S(1)}, u32[]{:S(2)}, u32[]{:S(2)}) collective-permute-start(bf16[64,512]{1,0:T(8,128)(2,1)S(1)} %start.1.refs_0_), channel_id=1, source_target_pairs={{0,16},{8,24},{16,0},{24,8},{1,17},{9,25},{17,1},{25,9},{2,18},{10... | collective-permute-start | bytes 196616 | tf_op jit(solution)/shard_map/ppermute | solution.py:305
  6.1 5.2 %collective-permute-start = (bf16[64,512]{1,0:T(8,128)(2,1)S(1)}, bf16[64,512]{1,0:T(8,128)(2,1)S(1)}, u32[]{:S(2)}, u32[]{:S(2)}) collective-permute-start(bf16[64,512]{1,0:T(8,128)(2,1)S(1)} %start.1.refs_0_), channel_id=1, source_target_pairs={{0,8},{8,16},{16,24},{24,0},{1,9},{9,17},{17,25},{25,1},{2,10},{10... | collective-permute-start | bytes 196616 | tf_op jit(solution)/shard_map/ppermute | solution.py:305
  17.2 5.8 %collective-permute-start.4 = (bf16[64,256]{1,0:T(8,128)(2,1)S(1)}, bf16[64,256]{1,0:T(8,128)(2,1)S(1)}, u32[]{:S(2)}, u32[]{:S(2)}) collective-permute-start(bf16[64,256]{1,0:T(8,128)(2,1)S(1)} %get-tuple-element.34), channel_id=1, source_target_pairs={{0,2},{1,3},{2,4},{3,5},{4,6},{5,7},{6,0},{7,1},{8,10},{9,11},{10,... | collective-permute-start | bytes 98312 | tf_op jit(solution)/shard_map/ppermute | solution.py:305
  18.4 5.7 %collective-permute-start.5 = (bf16[64,256]{1,0:T(8,128)(2,1)S(1)}, bf16[64,256]{1,0:T(8,128)(2,1)S(1)}, u32[]{:S(2)}, u32[]{:S(2)}) collective-permute-start(bf16[64,256]{1,0:T(8,128)(2,1)S(1)} %get-tuple-element.35), channel_id=1, source_target_pairs={{0,4},{1,5},{2,6},{3,7},{4,0},{5,1},{6,2},{7,3},{8,12},{9,13},{10,... | collective-permute-start | bytes 98312 | tf_op jit(solution)/shard_map/ppermute | solution.py:305
  21.4 3.9 %collective-permute-start.6 = (bf16[64,256]{1,0:T(8,128)(2,1)S(1)}, bf16[64,256]{1,0:T(8,128)(2,1)S(1)}, u32[]{:S(2)}, u32[]{:S(2)}) collective-permute-start(bf16[64,256]{1,0:T(8,128)(2,1)S(1)} %get-tuple-element.36), channel_id=1, source_target_pairs={{0,6},{1,7},{2,0},{3,1},{4,2},{5,3},{6,4},{7,5},{8,14},{9,15},{10,... | collective-permute-start | bytes 98312 | tf_op jit(solution)/shard_map/ppermute | solution.py:305
  25.4 4.0 %collective-permute-start.9 = (bf16[64,256]{1,0:T(8,128)(2,1)S(1)}, bf16[64,256]{1,0:T(8,128)(2,1)S(1)}, u32[]{:S(2)}, u32[]{:S(2)}) collective-permute-start(bf16[64,256]{1,0:T(8,128)(2,1)S(1)} %query.2.refs_0_), channel_id=1, source_target_pairs={{0,6},{1,7},{2,0},{3,1},{4,2},{5,3},{6,4},{7,5},{8,14},{9,15},{10,... | collective-permute-start | bytes 98312 | tf_op jit(solution)/shard_map/ppermute | solution.py:305
  27.7 4.8 %collective-permute-start.8 = (bf16[64,256]{1,0:T(8,128)(2,1)S(1)}, bf16[64,256]{1,0:T(8,128)(2,1)S(1)}, u32[]{:S(2)}, u32[]{:S(2)}) collective-permute-start(bf16[64,256]{1,0:T(8,128)(2,1)S(1)} %query.2.refs_0_), channel_id=1, source_target_pairs={{0,4},{1,5},{2,6},{3,7},{4,0},{5,1},{6,2},{7,3},{8,12},{9,13},{10,... | collective-permute-start | bytes 98312 | tf_op jit(solution)/shard_map/ppermute | solution.py:305
  27.7 5.7 %collective-permute-start.7 = (bf16[64,256]{1,0:T(8,128)(2,1)S(1)}, bf16[64,256]{1,0:T(8,128)(2,1)S(1)}, u32[]{:S(2)}, u32[]{:S(2)}) collective-permute-start(bf16[64,256]{1,0:T(8,128)(2,1)S(1)} %query.2.refs_0_), channel_id=1, source_target_pairs={{0,2},{1,3},{2,4},{3,5},{4,6},{5,7},{6,0},{7,1},{8,10},{9,11},{10,... | collective-permute-start | bytes 98312 | tf_op jit(solution)/shard_map/ppermute | solution.py:305
  36.7 7.1 %collective-permute-start.11 = (f32[64,512]{1,0:T(8,128)S(1)}, f32[64,512]{1,0:T(8,128)S(1)}, u32[]{:S(2)}, u32[]{:S(2)}) collective-permute-start(f32[64,512]{1,0:T(8,128)S(1)} %get-tuple-element.40), channel_id=1, source_target_pairs={{0,8},{8,16},{16,24},{24,0},{1,9},{9,17},{17,25},{25,1},{2,10},{10... | collective-permute-start | bytes 393224 | tf_op jit(solution)/shard_map/ppermute | solution.py:305
  36.9 7.9 %collective-permute-start.12 = (f32[64,512]{1,0:T(8,128)S(1)}, f32[64,512]{1,0:T(8,128)S(1)}, u32[]{:S(2)}, u32[]{:S(2)}) collective-permute-start(f32[64,512]{1,0:T(8,128)S(1)} %get-tuple-element.41), channel_id=1, source_target_pairs={{0,16},{8,24},{16,0},{24,8},{1,17},{9,25},{17,1},{25,9},{2,18},{10... | collective-permute-start | bytes 393224 | tf_op jit(solution)/shard_map/ppermute | solution.py:305
  38.5 7.5 %collective-permute-start.13 = (f32[64,512]{1,0:T(8,128)S(1)}, f32[64,512]{1,0:T(8,128)S(1)}, u32[]{:S(2)}, u32[]{:S(2)}) collective-permute-start(f32[64,512]{1,0:T(8,128)S(1)} %get-tuple-element.42), channel_id=1, source_target_pairs={{0,24},{8,0},{16,8},{24,16},{1,25},{9,1},{17,9},{25,17},{2,26},{10... | collective-permute-start | bytes 393224 | tf_op jit(solution)/shard_map/ppermute | solution.py:305
  46.0 6.2 %collective-permute-start.16 = (f32[64,512]{1,0:T(8,128)S(1)}, f32[64,512]{1,0:T(8,128)S(1)}, u32[]{:S(2)}, u32[]{:S(2)}) collective-permute-start(f32[64,512]{1,0:T(8,128)S(1)} %lift.2.refs_0_), channel_id=1, source_target_pairs={{0,24},{8,0},{16,8},{24,16},{1,25},{9,1},{17,9},{25,17},{2,26},{10... | collective-permute-start | bytes 393224 | tf_op jit(solution)/shard_map/ppermute | solution.py:305
  47.6 7.7 %collective-permute-start.15 = (f32[64,512]{1,0:T(8,128)S(1)}, f32[64,512]{1,0:T(8,128)S(1)}, u32[]{:S(2)}, u32[]{:S(2)}) collective-permute-start(f32[64,512]{1,0:T(8,128)S(1)} %lift.2.refs_0_), channel_id=1, source_target_pairs={{0,16},{8,24},{16,0},{24,8},{1,17},{9,25},{17,1},{25,9},{2,18},{10... | collective-permute-start | bytes 393224 | tf_op jit(solution)/shard_map/ppermute | solution.py:305
  49.2 6.1 %collective-permute-start.14 = (f32[64,512]{1,0:T(8,128)S(1)}, f32[64,512]{1,0:T(8,128)S(1)}, u32[]{:S(2)}, u32[]{:S(2)}) collective-permute-start(f32[64,512]{1,0:T(8,128)S(1)} %lift.2.refs_0_), channel_id=1, source_target_pairs={{0,8},{8,16},{16,24},{24,0},{1,9},{9,17},{17,25},{25,1},{2,10},{10... | collective-permute-start | bytes 393224 | tf_op jit(solution)/shard_map/ppermute | solution.py:305
  57.1 6.4 %collective-permute-start.20 = (f32[64,64]{1,0:T(8,128)S(1)}, f32[64,64]{1,0:T(8,128)S(1)}, u32[]{:S(2)}, u32[]{:S(2)}) collective-permute-start(f32[64,64]{1,0:T(8,128)S(1)} %sum.3.refs_0_), channel_id=1, source_target_pairs={{0,6},{1,7},{2,0},{3,1},{4,2},{5,3},{6,4},{7,5},{8,14},{9,15},{10,... | collective-permute-start | bytes 49160 | tf_op jit(solution)/shard_map/ppermute | solution.py:305
  58.1 5.5 %collective-permute-start.19 = (f32[64,64]{1,0:T(8,128)S(1)}, f32[64,64]{1,0:T(8,128)S(1)}, u32[]{:S(2)}, u32[]{:S(2)}) collective-permute-start(f32[64,64]{1,0:T(8,128)S(1)} %sum.3.refs_0_), channel_id=1, source_target_pairs={{0,4},{1,5},{2,6},{3,7},{4,0},{5,1},{6,2},{7,3},{8,12},{9,13},{10,... | collective-permute-start | bytes 49160 | tf_op jit(solution)/shard_map/ppermute | solution.py:305
  58.9 5.7 %collective-permute-start.18 = (f32[64,64]{1,0:T(8,128)S(1)}, f32[64,64]{1,0:T(8,128)S(1)}, u32[]{:S(2)}, u32[]{:S(2)}) collective-permute-start(f32[64,64]{1,0:T(8,128)S(1)} %sum.3.refs_0_), channel_id=1, source_target_pairs={{0,2},{1,3},{2,4},{3,5},{4,6},{5,7},{6,0},{7,1},{8,10},{9,11},{10,... | collective-permute-start | bytes 49160 | tf_op jit(solution)/shard_map/ppermute | solution.py:305
  70.2 6.0 %collective-permute-start.22 = (bf16[64,256]{1,0:T(8,128)(2,1)S(1)}, bf16[64,256]{1,0:T(8,128)(2,1)S(1)}, u32[]{:S(2)}, u32[]{:S(2)}) collective-permute-start(bf16[64,256]{1,0:T(8,128)(2,1)S(1)} %get-tuple-element.48), channel_id=1, source_target_pairs={{0,2},{1,3},{2,4},{3,5},{4,6},{5,7},{6,0},{7,1},{8,10},{9,11},{10,... | collective-permute-start | bytes 98312 | tf_op jit(solution)/shard_map/ppermute | solution.py:305
  70.4 5.8 %collective-permute-start.23 = (bf16[64,256]{1,0:T(8,128)(2,1)S(1)}, bf16[64,256]{1,0:T(8,128)(2,1)S(1)}, u32[]{:S(2)}, u32[]{:S(2)}) collective-permute-start(bf16[64,256]{1,0:T(8,128)(2,1)S(1)} %get-tuple-element.49), channel_id=1, source_target_pairs={{0,4},{1,5},{2,6},{3,7},{4,0},{5,1},{6,2},{7,3},{8,12},{9,13},{10,... | collective-permute-start | bytes 98312 | tf_op jit(solution)/shard_map/ppermute | solution.py:305
  71.8 4.7 %collective-permute-start.24 = (bf16[64,256]{1,0:T(8,128)(2,1)S(1)}, bf16[64,256]{1,0:T(8,128)(2,1)S(1)}, u32[]{:S(2)}, u32[]{:S(2)}) collective-permute-start(bf16[64,256]{1,0:T(8,128)(2,1)S(1)} %get-tuple-element.50), channel_id=1, source_target_pairs={{0,6},{1,7},{2,0},{3,1},{4,2},{5,3},{6,4},{7,5},{8,14},{9,15},{10,... | collective-permute-start | bytes 98312 | tf_op jit(solution)/shard_map/ppermute | solution.py:305
  76.5 4.9 %collective-permute-start.27 = (bf16[64,256]{1,0:T(8,128)(2,1)S(1)}, bf16[64,256]{1,0:T(8,128)(2,1)S(1)}, u32[]{:S(2)}, u32[]{:S(2)}) collective-permute-start(bf16[64,256]{1,0:T(8,128)(2,1)S(1)} %query.3.refs_0_), channel_id=1, source_target_pairs={{0,6},{1,7},{2,0},{3,1},{4,2},{5,3},{6,4},{7,5},{8,14},{9,15},{10,... | collective-permute-start | bytes 98312 | tf_op jit(solution)/shard_map/ppermute | solution.py:305
  79.9 4.8 %collective-permute-start.26 = (bf16[64,256]{1,0:T(8,128)(2,1)S(1)}, bf16[64,256]{1,0:T(8,128)(2,1)S(1)}, u32[]{:S(2)}, u32[]{:S(2)}) collective-permute-start(bf16[64,256]{1,0:T(8,128)(2,1)S(1)} %query.3.refs_0_), channel_id=1, source_target_pairs={{0,4},{1,5},{2,6},{3,7},{4,0},{5,1},{6,2},{7,3},{8,12},{9,13},{10,... | collective-permute-start | bytes 98312 | tf_op jit(solution)/shard_map/ppermute | solution.py:305
  80.1 5.7 %collective-permute-start.25 = (bf16[64,256]{1,0:T(8,128)(2,1)S(1)}, bf16[64,256]{1,0:T(8,128)(2,1)S(1)}, u32[]{:S(2)}, u32[]{:S(2)}) collective-permute-start(bf16[64,256]{1,0:T(8,128)(2,1)S(1)} %query.3.refs_0_), channel_id=1, source_target_pairs={{0,2},{1,3},{2,4},{3,5},{4,6},{5,7},{6,0},{7,1},{8,10},{9,11},{10,... | collective-permute-start | bytes 98312 | tf_op jit(solution)/shard_map/ppermute | solution.py:305
  89.1 7.1 %collective-permute-start.29 = (f32[64,512]{1,0:T(8,128)S(1)}, f32[64,512]{1,0:T(8,128)S(1)}, u32[]{:S(2)}, u32[]{:S(2)}) collective-permute-start(f32[64,512]{1,0:T(8,128)S(1)} %get-tuple-element.52), channel_id=1, source_target_pairs={{0,8},{8,16},{16,24},{24,0},{1,9},{9,17},{17,25},{25,1},{2,10},{10... | collective-permute-start | bytes 393224 | tf_op jit(solution)/shard_map/ppermute | solution.py:305
  89.6 7.8 %collective-permute-start.30 = (f32[64,512]{1,0:T(8,128)S(1)}, f32[64,512]{1,0:T(8,128)S(1)}, u32[]{:S(2)}, u32[]{:S(2)}) collective-permute-start(f32[64,512]{1,0:T(8,128)S(1)} %get-tuple-element.53), channel_id=1, source_target_pairs={{0,16},{8,24},{16,0},{24,8},{1,17},{9,25},{17,1},{25,9},{2,18},{10... | collective-permute-start | bytes 393224 | tf_op jit(solution)/shard_map/ppermute | solution.py:305
  90.4 7.2 %collective-permute-start.31 = (f32[64,512]{1,0:T(8,128)S(1)}, f32[64,512]{1,0:T(8,128)S(1)}, u32[]{:S(2)}, u32[]{:S(2)}) collective-permute-start(f32[64,512]{1,0:T(8,128)S(1)} %get-tuple-element.54), channel_id=1, source_target_pairs={{0,24},{8,0},{16,8},{24,16},{1,25},{9,1},{17,9},{25,17},{2,26},{10... | collective-permute-start | bytes 393224 | tf_op jit(solution)/shard_map/ppermute | solution.py:305
  97.9 4.2 %collective-permute-start.34 = (f32[64,64]{1,0:T(8,128)S(1)}, f32[64,64]{1,0:T(8,128)S(1)}, u32[]{:S(2)}, u32[]{:S(2)}) collective-permute-start(f32[64,64]{1,0:T(8,128)S(1)} %get-tuple-element.55.refs_0_), channel_id=1, source_target_pairs={{0,24},{8,0},{16,8},{24,16},{1,25},{9,1},{17,9},{25,17},{2,26},{10... | collective-permute-start | bytes 49160 | tf_op jit(solution)/shard_map/ppermute | solution.py:305
  100.2 3.9 %collective-permute-start.33 = (f32[64,64]{1,0:T(8,128)S(1)}, f32[64,64]{1,0:T(8,128)S(1)}, u32[]{:S(2)}, u32[]{:S(2)}) collective-permute-start(f32[64,64]{1,0:T(8,128)S(1)} %get-tuple-element.55.refs_0_), channel_id=1, source_target_pairs={{0,16},{8,24},{16,0},{24,8},{1,17},{9,25},{17,1},{25,9},{2,18},{10... | collective-permute-start | bytes 49160 | tf_op jit(solution)/shard_map/ppermute | solution.py:305
  101.1 4.8 %collective-permute-start.32 = (f32[64,64]{1,0:T(8,128)S(1)}, f32[64,64]{1,0:T(8,128)S(1)}, u32[]{:S(2)}, u32[]{:S(2)}) collective-permute-start(f32[64,64]{1,0:T(8,128)S(1)} %get-tuple-element.55.refs_0_), channel_id=1, source_target_pairs={{0,8},{8,16},{16,24},{24,0},{1,9},{9,17},{17,25},{25,1},{2,10},{10... | collective-permute-start | bytes 49160 | tf_op jit(solution)/shard_map/ppermute | solution.py:305
  107.9 4.9 %collective-permute-start.37 = (f32[64,64]{1,0:T(8,128)S(1)}, f32[64,64]{1,0:T(8,128)S(1)}, u32[]{:S(2)}, u32[]{:S(2)}) collective-permute-start(f32[64,64]{1,0:T(8,128)S(1)} %sum.5.refs_0_), channel_id=1, source_target_pairs={{0,4},{1,5},{2,6},{3,7},{4,0},{5,1},{6,2},{7,3},{8,12},{9,13},{10,... | collective-permute-start | bytes 49160 | tf_op jit(solution)/shard_map/ppermute | solution.py:305
  108.8 5.7 %collective-permute-start.36 = (f32[64,64]{1,0:T(8,128)S(1)}, f32[64,64]{1,0:T(8,128)S(1)}, u32[]{:S(2)}, u32[]{:S(2)}) collective-permute-start(f32[64,64]{1,0:T(8,128)S(1)} %sum.5.refs_0_), channel_id=1, source_target_pairs={{0,2},{1,3},{2,4},{3,5},{4,6},{5,7},{6,0},{7,1},{8,10},{9,11},{10,... | collective-permute-start | bytes 49160 | tf_op jit(solution)/shard_map/ppermute | solution.py:305
  (11 other events, 91.8 us)
